TPU v7x, 32 devices: a whole 2x2x4 slice. The times are simulated.
32 devices in a mesh: dp: 16 (over z, y, core), tensor: 2 (over x).
Axes of the slice: x: 2, y: 2, z: 4, core: 2. Of those that a mesh axis runs over, the one named last changes fastest.
Arguments:
- inputs: float32 [4096, 1024], P('dp', 'tensor'), may hold values from -6 to 6
- cotangent: float32 [4096, 1024], P('dp', 'tensor'), may hold values from -0.12 to 0.12
- gate_weight: float32 [1024, 4096], P('dp', 'tensor'), may hold values from -0.1875 to 0.1875
- up_weight: float32 [1024, 4096], P('dp', 'tensor'), may hold values from -0.1875 to 0.1875
- down_weight: float32 [1024, 4096], P('dp', 'tensor'), may hold values from -0.09375 to 0.09375
- gate_first: float32 [1024, 4096], P('dp', 'tensor'), may hold values from -6 to 6
- gate_second: float32 [1024, 4096], P('dp', 'tensor'), may hold values from 0.5 to 4
- up_first: float32 [1024, 4096], P('dp', 'tensor'), may hold values from -6 to 6
- up_second: float32 [1024, 4096], P('dp', 'tensor'), may hold values from 0.5 to 4
Outputs:
- gate_new: float32 [1024, 4096], P('dp', 'tensor')
- gate_first_new: float32 [1024, 4096], P('dp', 'tensor')
- gate_second_new: float32 [1024, 4096], P('dp', 'tensor')
- up_new: float32 [1024, 4096], P('dp', 'tensor')
- up_first_new: float32 [1024, 4096], P('dp', 'tensor')
- up_second_new: float32 [1024, 4096], P('dp', 'tensor')
All inputs are finite; a program needn't handle non-finite values.
Results may differ from a plain program's by a relative error of at most 0.00005.
Values sent between devices are 32-bit elements; how exact they have to be, the bound alone decides.
No kernel may reach another device: no remote copies, remote signals or barrier semaphores. Data moves between devices by JAX's collectives and lax.ppermute only.
A program may use at most 64 MiB of HBM per device.

v0:
```python
import functools

import jax
import jax.numpy as jnp
from jax import lax
from jax.experimental import pallas as pl
from jax.experimental.pallas import tpu as pltpu
from jax.sharding import PartitionSpec as P

STEP = 100
CHUNKS = 4
VMEM_LIMIT = 60 * 1024 * 1024


def adam_update(weight, first, second, grad):
    first_new = 0.9 * first + 0.1 * grad
    second_new = 0.95 * second + 0.05 * grad * grad
    first_hat = first_new / (1.0 - 0.9**STEP)
    second_hat = second_new / (1.0 - 0.95**STEP)
    weight_new = weight - 0.003 * first_hat / (jnp.sqrt(second_hat) + 1e-08)
    return (weight_new, first_new, second_new)


class Bit:
    def __init__(self, axis, size, place):
        self.axis = axis
        self.pairs = [(i, i ^ (1 << place)) for i in range(size)]
        self.mine = (lax.axis_index(axis) >> place) & 1

    def swap(self, array):
        return lax.ppermute(array, self.axis, self.pairs)

    def own(self, array, dim):
        return lax.dynamic_index_in_dim(array, self.mine, dim, keepdims=False)

    def other(self, array, dim):
        return lax.dynamic_index_in_dim(array, 1 - self.mine, dim, keepdims=False)

    def ordered(self, own, received, dim):
        low = jnp.where(self.mine == 0, own, received)
        high = jnp.where(self.mine == 0, received, own)
        return jnp.stack([low, high], dim)

    def joined(self, own, received, dim):
        low = jnp.where(self.mine == 0, own, received)
        high = jnp.where(self.mine == 0, received, own)
        return jnp.concatenate([low, high], dim)


def parts_of(x):
    high = x.astype(jnp.bfloat16)
    return high, (x - high.astype(jnp.float32)).astype(jnp.bfloat16)


def product(left, right, left_dim):
    dims = (((left_dim,), (0,)), ((), ()))
    dot = functools.partial(
        lax.dot_general, dimension_numbers=dims, preferred_element_type=jnp.float32
    )
    return dot(left[0], right[0]) + (dot(left[0], right[1]) + dot(left[1], right[0]))


def chunk_kernel(starts, width, mine_ref, *refs):
    sources, (keep_ref, send_ref) = refs[:20], refs[20:22]
    held, piece, up_high, up_low, down_high, down_low, total, done = refs[22:]
    side, core, far = mine_ref[0], mine_ref[1], mine_ref[2]
    _, blocks, _, depth, _ = piece.shape
    half = held.shape[2]

    copies = []
    for i, start in enumerate(starts):
        source = sources[16 + i].at[:, :, :, pl.ds(start, width)]
        copies.append(pltpu.make_async_copy(source, piece.at[i], done.at[i]))
    for b in range(4):
        for i in (2 * b, 2 * b + 1, 8 + 2 * b, 9 + 2 * b):
            copies.append(pltpu.make_async_copy(sources[i], held.at[i], done.at[4 + i]))
    for copy in copies:
        copy.start()

    for i, (place, bit) in enumerate(
        ((far, core), (far, 1 - core), (1 - far, core), (1 - far, 1 - core))
    ):
        copies[i].wait()
        for block in range(blocks):
            row = pl.multiple_of(((place * blocks + block) * 2 + bit) * depth, depth)
            for k in range(3):
                high, low = parts_of(piece[i, block, k])
                if k < 2:
                    up_high[pl.ds(row, depth), k * width : (k + 1) * width] = high
                    up_low[pl.ds(row, depth), k * width : (k + 1) * width] = low
                else:
                    down_high[pl.ds(row, depth), :] = high
                    down_low[pl.ds(row, depth), :] = low

    at = [pl.ds(pl.multiple_of(h * half, half), half) for h in (side, 1 - side)]
    for b in range(4):
        for copy in copies[4 + 4 * b : 8 + 4 * b]:
            copy.wait()
        pieces = [parts_of(held[2 * b + h]) for h in range(2)]
        sums = sum(product(pieces[h], (up_high[at[h], :], up_low[at[h], :]), 1) for h in range(2))
        back = sum(
            product(
                parts_of(held[8 + 2 * b + h]), (down_high[at[h], :], down_low[at[h], :]), 1
            )
            for h in range(2)
        )
        gate, lift = sums[:, :width], sums[:, width:]
        sigmoid = 1.0 / (1.0 + jnp.exp(-gate))
        back = back * sigmoid
        grads = parts_of(
            jnp.concatenate([back * lift * (1.0 + gate * (1.0 - sigmoid)), back * gate], 1)
        )
        for h in range(2):
            term = product(grads, pieces[h], 0)
            total[h] = term if b == 0 else total[h] + term

    for h, place in ((0, side), (1, 1 - side)):
        turned = total[h].T
        for bit in range(2):
            for ref, whose in ((keep_ref, bit), (send_ref, 1 - bit)):

                @pl.when(core == whose)
                def _():
                    for block in range(blocks):
                        start = (block * 2 + bit) * depth
                        ref[place * blocks + block] = turned[start : start + depth, :]


def after(tree):
    leaves, shape = jax.tree.flatten(tree)
    return jax.tree.unflatten(shape, lax.optimization_barrier(leaves))


def make_local(n_dp, n_tensor):
    n_bits = n_dp.bit_length() - 1
    t_bits = n_tensor.bit_length() - 1

    def local(
        inputs,
        cotangent,
        gate_weight,
        up_weight,
        down_weight,
        gate_first,
        gate_second,
        up_first,
        up_second,
    ):
        bits = [Bit("dp", n_dp, place) for place in reversed(range(n_bits))]
        far, near, core = bits[0], bits[-2], bits[-1]
        middle = bits[1:-2]
        features = [Bit("tensor", n_tensor, place) for place in range(t_bits)]
        side = features[-1]
        depth, columns = gate_weight.shape
        part = columns // 4
        chunks = CHUNKS if part % (CHUNKS * 128) == 0 else 1
        width = part // chunks
        both = 2 * width
        half = (chunks + 1) // 2 * width
        most = (chunks - chunks // 4) * width
        for bit in features[:-1]:
            inputs = bit.joined(inputs, bit.swap(inputs), 1)
            cotangent = bit.joined(cotangent, bit.swap(cotangent), 1)

        def columns_of(far_bit, near_bit):
            start = (far_bit * 2 + near_bit) * part
            return jnp.stack(
                [
                    lax.dynamic_slice_in_dim(weight, start, part, 1)
                    for weight in (gate_weight, up_weight, down_weight)
                ]
            )

        def over_middle(pair):
            moved = [pair]
            for bit in reversed(middle):
                moved = moved + [[bit.swap(x) for x in p] for p in moved]
            return moved

        def arranged(moved):
            blocks = [near.ordered(p[0], p[1], 0) for p in moved]
            for bit in middle:
                half_way = len(blocks) // 2
                blocks = [
                    bit.ordered(a, b, 0) for a, b in zip(blocks[:half_way], blocks[half_way:])
                ]
            return blocks[0].reshape((-1,) + blocks[0].shape[-3:])

        tokens = inputs.shape[0]

        oo = columns_of(far.mine, near.mine)
        ox = columns_of(far.mine, 1 - near.mine)
        s = after(
            dict(
                in_far=far.swap(inputs),
                in_side=side.swap(inputs),
                cot_side=side.swap(cotangent),
                oo_near=near.swap(ox),
                in_near=near.swap(inputs),
                inputs=inputs,
                cotangent=cotangent,
                oo=oo,
                xo=columns_of(1 - far.mine, near.mine),
                xx=columns_of(1 - far.mine, 1 - near.mine),
            )
        )

        n_weight = 3 * depth * part // cotangent.shape[1]
        by_near = jnp.concatenate([s["xx"].reshape(n_weight, -1), s["cotangent"]], 0)
        by_near = near.swap(by_near)
        s = after(
            dict(
                s,
                cot_far=far.swap(s["cotangent"]),
                in_far_side=side.swap(s["in_far"]),
                in_diag=side.swap(s["in_near"]),
                xo_near=by_near[:n_weight].reshape(3, depth, part),
                cot_near=by_near[n_weight:],
                kept=over_middle([s["oo"]]),
            )
        )

        by_far = far.swap(jnp.stack([s["xo"][..., :most], s["xo_near"][..., :most]]))
        by_near = near.swap(jnp.concatenate([s["in_far"], s["cot_far"]], 0))
        s = after(
            dict(
                s,
                come=by_far,
                send=jnp.stack([s["xo"][..., most:], s["xo_near"][..., most:]]),
                cot_diag=side.swap(s["cot_near"]),
                cot_far_side=side.swap(s["cot_far"]),
                in_far_near=by_near[:tokens],
                cot_far_near=by_near[tokens:],
                kept_near=over_middle([s["oo_near"]]),
            )
        )

        late = s["come"][..., half:]
        if most < part:
            late = (late, far.swap(s["send"]))
        kept = arranged([a + b for a, b in zip(s["kept"], s["kept_near"])])
        s = after(
            dict(
                s,
                late=late,
                in_far_diag=near.swap(s["in_far_side"]),
                cot_far_diag=side.swap(s["cot_far_near"]),
                kept=kept,
                kept_core=core.swap(kept),
                come=over_middle([s["come"][..., :half]]),
            )
        )
        come = arranged([[p[0][0], p[0][1]] for p in s["come"]])
        s = after(dict(s, come=come, come_core=core.swap(come)))
        tokens_of = [
            s[name]
            for name in (
                "inputs", "in_side", "in_near", "in_diag",
                "in_far", "in_far_side", "in_far_near", "in_far_diag",
                "cotangent", "cot_side", "cot_near", "cot_diag",
                "cot_far", "cot_far_side", "cot_far_near", "cot_far_diag",
            )
        ]
        mine = jnp.stack([side.mine, core.mine, far.mine]).astype(jnp.int32)

        def grads_of(ahead, kept_at, come_at, *arrays):
            feature_rows = n_dp * depth
            out = jax.ShapeDtypeStruct((n_dp // 2, depth, both), jnp.float32)
            vmem = pl.BlockSpec(memory_space=pltpu.VMEM)
            any_space = pl.BlockSpec(memory_space=pl.ANY)
            starts = (kept_at, kept_at, come_at, come_at)
            keep, send = pl.pallas_call(
                functools.partial(chunk_kernel, starts, width),
                out_shape=(out, out),
                in_specs=[pl.BlockSpec(memory_space=pltpu.SMEM)] + [any_space] * len(arrays),
                out_specs=(vmem, vmem),
                scratch_shapes=[
                    pltpu.VMEM((16,) + inputs.shape, jnp.float32),
                    pltpu.VMEM((4, n_dp // 4, 3, depth, width), jnp.float32),
                    pltpu.VMEM((feature_rows, both), jnp.bfloat16),
                    pltpu.VMEM((feature_rows, both), jnp.bfloat16),
                    pltpu.VMEM((feature_rows, width), jnp.bfloat16),
                    pltpu.VMEM((feature_rows, width), jnp.bfloat16),
                    pltpu.VMEM((2, both, feature_rows // 2), jnp.float32),
                    pltpu.SemaphoreType.DMA((20,)),
                ],
                compiler_params=pltpu.CompilerParams(vmem_limit_bytes=VMEM_LIMIT),
                cost_estimate=pl.CostEstimate(
                    flops=24 * tokens * feature_rows * 5 * width // 2,
                    bytes_accessed=16 * tokens * feature_rows,
                    transcendentals=4 * tokens * width,
                ),
            )(mine, *arrays)
            shape = [2] * (n_bits - 1) + [depth, both]
            send, ahead = after((send, ahead))
            return (keep.reshape(shape), core.swap(send).reshape(shape)), ahead

        kept, kept_core = s["kept"], s["kept_core"]
        arrived = {0: (s["come"], s["come_core"])}
        late = s["late"]
        stages = {}
        fresh = None
        for step in range(chunks + 4):
            new = {}
            if step - 3 >= 0 and step - 3 < chunks:
                keep, send = stages[step - 3]
                new[step - 3] = near.ordered(keep, near.swap(send), 0)
            if step - 2 >= 0 and step - 2 < chunks:
                keep, send = stages[step - 2]
                grad = far.ordered(keep, far.swap(send), 1)
                new[step - 2] = (near.own(grad, 0), near.other(grad, 0))
            if step - 1 >= 0 and step - 1 < chunks:
                terms = stages[step - 1]
                for bit in middle:
                    keep, send = (sum(part(x, 1) for x in terms) for part in (bit.own, bit.other))
                    terms = (keep, bit.swap(send))
                grad = sum(terms)
                new[step - 1] = (far.own(grad, 0), far.other(grad, 0))
            if step == 0 and half < part:
                fresh = over_middle([jnp.concatenate(late, -1) if most < part else late])
            if step == 1 and half < part:
                fresh = arranged([[p[0][0], p[0][1]] for p in fresh])
                fresh = (fresh, core.swap(fresh))
            if step < chunks:
                group, start = (0, step * width) if step * width < half else (1, step * width - half)
                new[step], fresh = grads_of(
                    fresh, step * width, start, *tokens_of, kept, kept_core, *arrived[group]
                )
            stages.update(new)
            if step < chunks + 3:
                stages, kept, kept_core, tokens_of, fresh, arrived = after(
                    (stages, kept, kept_core, tokens_of, fresh, arrived)
                )
            if step == 1 and half < part:
                arrived[1] = fresh

        def assembled(which):
            return jnp.concatenate(
                [
                    stages[chunk][n, f, :, which * width : (which + 1) * width]
                    for f in range(2)
                    for n in range(2)
                    for chunk in range(chunks)
                ],
                1,
            )

        gate_new, gate_first_new, gate_second_new = adam_update(
            gate_weight, gate_first, gate_second, assembled(0)
        )
        up_new, up_first_new, up_second_new = adam_update(
            up_weight, up_first, up_second, assembled(1)
        )
        return (gate_new, gate_first_new, gate_second_new, up_new, up_first_new, up_second_new)

    return local


def solution(mesh):
    spec = P("dp", "tensor")
    local = make_local(mesh.shape["dp"], mesh.shape["tensor"])
    return jax.shard_map(
        local, mesh=mesh, in_specs=(spec,) * 9, out_specs=(spec,) * 6, check_vma=False
    )
```

profile of v0, /device:TPU:0, one launch (start us, length us, event | category | flops | bytes accessed | tf_op | source)
XLA Modules:
  0.0 205.1 jit_solution(6336195313862983099)
XLA Ops:
  0.6 3.0 %collective-permute-start.2 = (f32[256,512]{1,0:T(8,128)}, f32[256,512]{1,0:T(8,128)S(1)}, u32[]{:S(2)}, u32[]{:S(2)}) collective-permute-start(f32[256,512]{1,0:T(8,128)} %refs_0_.3), channel_id=1, source_target_pairs={{0,4},{2,6},{4,0},{6,2},{8,12},{10,14},{12,8},{14,10},{16,20},{18,... | collective-permute-start | bytes 1572872 | tf_op jit(solution)/shard_map/ppermute | solution.py:31
  3.7 2.6 %collective-permute-start.1 = (f32[256,512]{1,0:T(8,128)}, f32[256,512]{1,0:T(8,128)S(1)}, u32[]{:S(2)}, u32[]{:S(2)}) collective-permute-start(f32[256,512]{1,0:T(8,128)} %refs_0_.3), channel_id=1, source_target_pairs={{0,16},{2,18},{4,20},{6,22},{8,24},{10,26},{12,28},{14,30},{16,0},... | collective-permute-start | bytes 1572872 | tf_op jit(solution)/shard_map/ppermute | solution.py:31
  11.2 13.0 %collective-permute-done.4 = f32[3,64,512]{2,1,0:T(8,128)S(1)} collective-permute-done((f32[3,64,512]{2,1,0:T(8,128)S(1)}, f32[3,64,512]{2,1,0:T(8,128)S(1)}, u32[]{:S(2)}, u32[]{:S(2)}) %collective-permute-start.4) | collective-permute-done | bytes 393248 | tf_op jit(solution)/shard_map/ppermute | solution.py:31
  24.2 6.6 %collective-permute-done.refs_9_ = f32[256,512]{1,0:T(8,128)S(1)} collective-permute-done((f32[256,512]{1,0:T(8,128)}, f32[256,512]{1,0:T(8,128)S(1)}, u32[]{:S(2)}, u32[]{:S(2)}) %collective-permute-start) | collective-permute-done | bytes 524320 | tf_op jit(solution)/shard_map/ppermute | solution.py:31
  34.9 2.3 %collective-permute-start.9 = (f32[3,64,512]{2,1,0:T(8,128)}, f32[3,64,512]{2,1,0:T(8,128)}, u32[]{:S(2)}, u32[]{:S(2)}) collective-permute-start(f32[3,64,512]{2,1,0:T(8,128)} %pad_maximum_fusion.8), channel_id=1, source_target_pairs={{0,8},{2,10},{4,12},{6,14},{8,0},{10,2},{12,4},{14,6},{16,24},{18,... | collective-permute-start | bytes 1179656 | tf_op jit(solution)/shard_map/ppermute | solution.py:31
  37.1 15.8 %collective-permute-done.6 = f32[448,512]{1,0:T(8,128)} collective-permute-done((f32[448,512]{1,0:T(8,128)}, f32[448,512]{1,0:T(8,128)}, u32[]{:S(2)}, u32[]{:S(2)}) %collective-permute-start.6) | collective-permute-done | bytes 917536 | tf_op jit(solution)/shard_map/ppermute | solution.py:31
  55.8 2.3 %collective-permute-done.5.refs_12_ = f32[256,512]{1,0:T(8,128)S(1)} collective-permute-done((f32[256,512]{1,0:T(8,128)S(1)}, f32[256,512]{1,0:T(8,128)S(1)}, u32[]{:S(2)}, u32[]{:S(2)}) %collective-permute-start.5) | collective-permute-done | bytes 524320 | tf_op jit(solution)/shard_map/ppermute | solution.py:31
  64.1 19.4 %collective-permute-done.12 = f32[512,512]{1,0:T(8,128)S(1)} collective-permute-done((f32[512,512]{1,0:T(8,128)S(1)}, f32[512,512]{1,0:T(8,128)S(1)}, u32[]{:S(2)}, u32[]{:S(2)}) %collective-permute-start.12) | collective-permute-done | bytes 1048608 | tf_op jit(solution)/shard_map/ppermute | solution.py:31
  84.3 4.7 %collective-permute-done.10 = f32[2,3,64,384]{3,2,1,0:T(8,128)S(1)} collective-permute-done((f32[2,3,64,384]{3,2,1,0:T(8,128)S(1)}, f32[2,3,64,384]{3,2,1,0:T(8,128)S(1)}, u32[]{:S(2)}, u32[]{:S(2)}) %collective-permute-start.10) | collective-permute-done | bytes 589856 | tf_op jit(solution)/shard_map/ppermute | solution.py:31
  94.0 2.9 %collective-permute-start.19 = (f32[2,3,64,128]{3,2,1,0:T(8,128)S(1)}, f32[2,3,64,128]{3,2,1,0:T(8,128)S(1)}, u32[]{:S(2)}, u32[]{:S(2)}) collective-permute-start(f32[2,3,64,128]{3,2,1,0:T(8,128)S(1)} %pad_maximum_fusion.20), channel_id=1, source_target_pairs={{0,16},{2,18},{4,20},{6,22},{8,24},{10,26},{12,28},{14,30},{16,0},... | collective-permute-start | bytes 589832 | tf_op jit(solution)/shard_map/ppermute | solution.py:31
  96.9 10.0 %collective-permute-done.19 = f32[2,3,64,128]{3,2,1,0:T(8,128)S(1)} collective-permute-done((f32[2,3,64,128]{3,2,1,0:T(8,128)S(1)}, f32[2,3,64,128]{3,2,1,0:T(8,128)S(1)}, u32[]{:S(2)}, u32[]{:S(2)}) %collective-permute-start.19) | collective-permute-done | bytes 196640 | tf_op jit(solution)/shard_map/ppermute | solution.py:31
  106.9 2.2 %collective-permute-done.15 = f32[2,3,64,256]{3,2,1,0:T(8,128)S(1)} collective-permute-done((f32[2,3,64,256]{3,2,1,0:T(8,128)S(1)}, f32[2,3,64,256]{3,2,1,0:T(8,128)S(1)}, u32[]{:S(2)}, u32[]{:S(2)}) %collective-permute-start.15) | collective-permute-done | bytes 393248 | tf_op jit(solution)/shard_map/ppermute | solution.py:31
  111.2 2.3 %collective-permute-done.20.refs_19_ = f32[4,3,64,256]{3,2,1,0:T(8,128)S(1)} collective-permute-done((f32[4,3,64,256]{3,2,1,0:T(8,128)S(1)}, f32[4,3,64,256]{3,2,1,0:T(8,128)S(1)}, u32[]{:S(2)}, u32[]{:S(2)}) %collective-permute-start.20) | collective-permute-done | bytes 786464 | tf_op jit(solution)/shard_map/ppermute | solution.py:31
  115.4 10.3 %shard_map.136 = (f32[8,64,256]{2,1,0:T(8,128)}, f32[8,64,256]{2,1,0:T(8,128)}) custom-call(s32[3]{0:T(128)} %pad_add_fusion.mine_ref, f32[256,512]{1,0:T(8,128)} %refs_0_.3, f32[256,512]{1,0:T(8,128)} %copy-done.8, f32[256,512]{1,0:T(8,128)} %copy-done.7, f32[256,512]{1,0:T(8,128)} %copy-done.10, f32[256,512]{1,0:T(8,128)} %copy-done.4, ...), custom_call_target="tpu_custom_call" | custom-call | flops 2013265920 | bytes 4194304 | tf_op jit(solution)/shard_map/pallas_call | solution.py:272
  125.7 2.1 %collective-permute-done.22 = f32[8,64,256]{2,1,0:T(8,128)S(1)} collective-permute-done((f32[8,64,256]{2,1,0:T(8,128)}, f32[8,64,256]{2,1,0:T(8,128)S(1)}, u32[]{:S(2)}, u32[]{:S(2)}) %collective-permute-start.22) | collective-permute-done | bytes 524320 | tf_op jit(solution)/shard_map/ppermute | solution.py:31
  130.6 10.4 %shard_map.137 = (f32[8,64,256]{2,1,0:T(8,128)}, f32[8,64,256]{2,1,0:T(8,128)}) custom-call(s32[3]{0:T(128)} %pad_add_fusion.mine_ref, f32[256,512]{1,0:T(8,128)} %refs_0_.3, f32[256,512]{1,0:T(8,128)} %copy-done.8, f32[256,512]{1,0:T(8,128)} %copy-done.7, f32[256,512]{1,0:T(8,128)} %copy-done.10, f32[256,512]{1,0:T(8,128)} %copy-done.4, ...), custom_call_target="tpu_custom_call" | custom-call | flops 2013265920 | bytes 4194304 | tf_op jit(solution)/shard_map/pallas_call | solution.py:272
  146.2 10.4 %shard_map.138 = (f32[8,64,256]{2,1,0:T(8,128)}, f32[8,64,256]{2,1,0:T(8,128)}) custom-call(s32[3]{0:T(128)} %pad_add_fusion.mine_ref, f32[256,512]{1,0:T(8,128)} %refs_0_.3, f32[256,512]{1,0:T(8,128)} %copy-done.8, f32[256,512]{1,0:T(8,128)} %copy-done.7, f32[256,512]{1,0:T(8,128)} %copy-done.10, f32[256,512]{1,0:T(8,128)} %copy-done.4, ...), custom_call_target="tpu_custom_call" | custom-call | flops 2013265920 | bytes 4194304 | tf_op jit(solution)/shard_map/pallas_call | solution.py:272
  162.5 10.2 %shard_map.139 = (f32[8,64,256]{2,1,0:T(8,128)}, f32[8,64,256]{2,1,0:T(8,128)}) custom-call(s32[3]{0:T(128)} %pad_add_fusion.mine_ref, f32[256,512]{1,0:T(8,128)} %refs_0_.3, f32[256,512]{1,0:T(8,128)} %copy-done.8, f32[256,512]{1,0:T(8,128)} %copy-done.7, f32[256,512]{1,0:T(8,128)} %copy-done.10, f32[256,512]{1,0:T(8,128)} %copy-done.4, ...), custom_call_target="tpu_custom_call" | custom-call | flops 2013265920 | bytes 4194304 | tf_op jit(solution)/shard_map/pallas_call | solution.py:272
  178.4 2.0 collective-permute-done.33
  180.4 4.0 %collective-permute-done.34 = f32[2,64,256]{2,1,0:T(8,128)S(1)} collective-permute-done((f32[2,64,256]{2,1,0:T(8,128)S(1)}, f32[2,64,256]{2,1,0:T(8,128)S(1)}, u32[]{:S(2)}, u32[]{:S(2)}) %collective-permute-start.34) | collective-permute-done | bytes 131104 | tf_op jit(solution)/shard_map/ppermute | solution.py:31
  184.5 2.6 %collective-permute-done.35 = f32[2,2,64,256]{3,2,1,0:T(8,128)S(1)} collective-permute-done((f32[2,2,64,256]{3,2,1,0:T(8,128)S(1)}, f32[2,2,64,256]{3,2,1,0:T(8,128)S(1)}, u32[]{:S(2)}, u32[]{:S(2)}) %collective-permute-start.35) | collective-permute-done | bytes 262176 | tf_op jit(solution)/shard_map/ppermute | solution.py:31
  190.0 2.3 %collective-permute-done.36 = f32[2,64,256]{2,1,0:T(8,128)S(1)} collective-permute-done((f32[2,64,256]{2,1,0:T(8,128)S(1)}, f32[2,64,256]{2,1,0:T(8,128)S(1)}, u32[]{:S(2)}, u32[]{:S(2)}) %collective-permute-start.36) | collective-permute-done | bytes 131104 | tf_op jit(solution)/shard_map/ppermute | solution.py:31
  192.3 4.0 %collective-permute-done.37 = f32[2,64,256]{2,1,0:T(8,128)S(1)} collective-permute-done((f32[2,64,256]{2,1,0:T(8,128)S(1)}, f32[2,64,256]{2,1,0:T(8,128)S(1)}, u32[]{:S(2)}, u32[]{:S(2)}) %collective-permute-start.37) | collective-permute-done | bytes 131104 | tf_op jit(solution)/shard_map/ppermute | solution.py:31
  197.0 4.5 %collective-permute-done.38 = f32[2,64,256]{2,1,0:T(8,128)S(1)} collective-permute-done((f32[2,64,256]{2,1,0:T(8,128)S(1)}, f32[2,64,256]{2,1,0:T(8,128)S(1)}, u32[]{:S(2)}, u32[]{:S(2)}) %collective-permute-start.38) | collective-permute-done | bytes 131104 | tf_op jit(solution)/shard_map/ppermute | solution.py:31
  (207 shorter events, 53.6 us)
Async XLA Ops:
  0.6 30.2 %collective-permute-start.2 = (f32[256,512]{1,0:T(8,128)}, f32[256,512]{1,0:T(8,128)S(1)}, u32[]{:S(2)}, u32[]{:S(2)}) collective-permute-start(f32[256,512]{1,0:T(8,128)} %refs_0_.3), channel_id=1, source_target_pairs={{0,4},{2,6},{4,0},{6,2},{8,12},{10,14},{12,8},{14,10},{16,20},{18,... | collective-permute-start | bytes 1572872 | tf_op jit(solution)/shard_map/ppermute | solution.py:31
  3.7 27.1 %collective-permute-start.1 = (f32[256,512]{1,0:T(8,128)}, f32[256,512]{1,0:T(8,128)S(1)}, u32[]{:S(2)}, u32[]{:S(2)}) collective-permute-start(f32[256,512]{1,0:T(8,128)} %refs_0_.3), channel_id=1, source_target_pairs={{0,16},{2,18},{4,20},{6,22},{8,24},{10,26},{12,28},{14,30},{16,0},... | collective-permute-start | bytes 1572872 | tf_op jit(solution)/shard_map/ppermute | solution.py:31
  6.3 24.6 %collective-permute-start.3 = (f32[256,512]{1,0:T(8,128)}, f32[256,512]{1,0:T(8,128)S(1)}, u32[]{:S(2)}, u32[]{:S(2)}) collective-permute-start(f32[256,512]{1,0:T(8,128)} %refs_0_.3), channel_id=1, source_target_pairs={{0,1},{1,0},{2,3},{3,2},{4,5},{5,4},{6,7},{7,6},{8,9},{9,8},{10,11... | collective-permute-start | bytes 1572872 | tf_op jit(solution)/shard_map/ppermute | solution.py:31
  7.8 23.1 %collective-permute-start = (f32[256,512]{1,0:T(8,128)}, f32[256,512]{1,0:T(8,128)S(1)}, u32[]{:S(2)}, u32[]{:S(2)}) collective-permute-start(f32[256,512]{1,0:T(8,128)} %refs_8_.3), channel_id=1, source_target_pairs={{0,1},{1,0},{2,3},{3,2},{4,5},{5,4},{6,7},{7,6},{8,9},{9,8},{10,11... | collective-permute-start | bytes 1572872 | tf_op jit(solution)/shard_map/ppermute | solution.py:31
  9.8 14.4 %collective-permute-start.4 = (f32[3,64,512]{2,1,0:T(8,128)S(1)}, f32[3,64,512]{2,1,0:T(8,128)S(1)}, u32[]{:S(2)}, u32[]{:S(2)}) collective-permute-start(f32[3,64,512]{2,1,0:T(8,128)S(1)} %pad_maximum_fusion.9), channel_id=1, source_target_pairs={{0,4},{2,6},{4,0},{6,2},{8,12},{10,14},{12,8},{14,10},{16,20},{18,... | collective-permute-start | bytes 1179656 | tf_op jit(solution)/shard_map/ppermute | solution.py:31
  32.1 20.9 %collective-permute-start.6 = (f32[448,512]{1,0:T(8,128)}, f32[448,512]{1,0:T(8,128)}, u32[]{:S(2)}, u32[]{:S(2)}) collective-permute-start(f32[448,512]{1,0:T(8,128)} %pad_maximum_fusion.2), channel_id=1, source_target_pairs={{0,4},{2,6},{4,0},{6,2},{8,12},{10,14},{12,8},{14,10},{16,20},{18,... | collective-permute-start | bytes 2752520 | tf_op jit(solution)/shard_map/ppermute | solution.py:31
  32.6 22.6 %collective-permute-start.7 = (f32[256,512]{1,0:T(8,128)S(1)}, f32[256,512]{1,0:T(8,128)S(1)}, u32[]{:S(2)}, u32[]{:S(2)}) collective-permute-start(f32[256,512]{1,0:T(8,128)S(1)} %collective-permute-done.2.refs_2_), channel_id=1, source_target_pairs={{0,1},{1,0},{2,3},{3,2},{4,5},{5,4},{6,7},{7,6},{8,9},{9,8},{10,11... | collective-permute-start | bytes 1572872 | tf_op jit(solution)/shard_map/ppermute | solution.py:31
  34.1 21.7 %collective-permute-start.8 = (f32[256,512]{1,0:T(8,128)S(1)}, f32[256,512]{1,0:T(8,128)}, u32[]{:S(2)}, u32[]{:S(2)}) collective-permute-start(f32[256,512]{1,0:T(8,128)S(1)} %collective-permute-done.1.refs_4_), channel_id=1, source_target_pairs={{0,1},{1,0},{2,3},{3,2},{4,5},{5,4},{6,7},{7,6},{8,9},{9,8},{10,11... | collective-permute-start | bytes 1572872 | tf_op jit(solution)/shard_map/ppermute | solution.py:31
  34.6 23.5 %collective-permute-start.5 = (f32[256,512]{1,0:T(8,128)S(1)}, f32[256,512]{1,0:T(8,128)S(1)}, u32[]{:S(2)}, u32[]{:S(2)}) collective-permute-start(f32[256,512]{1,0:T(8,128)S(1)} %copy-done.2), channel_id=1, source_target_pairs={{0,16},{2,18},{4,20},{6,22},{8,24},{10,26},{12,28},{14,30},{16,0},... | collective-permute-start | bytes 1572872 | tf_op jit(solution)/shard_map/ppermute | solution.py:31
  34.9 20.2 %collective-permute-start.9 = (f32[3,64,512]{2,1,0:T(8,128)}, f32[3,64,512]{2,1,0:T(8,128)}, u32[]{:S(2)}, u32[]{:S(2)}) collective-permute-start(f32[3,64,512]{2,1,0:T(8,128)} %pad_maximum_fusion.8), channel_id=1, source_target_pairs={{0,8},{2,10},{4,12},{6,14},{8,0},{10,2},{12,4},{14,6},{16,24},{18,... | collective-permute-start | bytes 1179656 | tf_op jit(solution)/shard_map/ppermute | solution.py:31
  58.1 26.2 %collective-permute-start.13 = (f32[256,512]{1,0:T(8,128)S(1)}, f32[256,512]{1,0:T(8,128)S(1)}, u32[]{:S(2)}, u32[]{:S(2)}) collective-permute-start(f32[256,512]{1,0:T(8,128)S(1)} %collective-permute-done.5.refs_12_), channel_id=1, source_target_pairs={{0,1},{1,0},{2,3},{3,2},{4,5},{5,4},{6,7},{7,6},{8,9},{9,8},{10,11... | collective-permute-start | bytes 1572872 | tf_op jit(solution)/shard_map/ppermute | solution.py:31
  59.6 23.8 %collective-permute-start.12 = (f32[512,512]{1,0:T(8,128)S(1)}, f32[512,512]{1,0:T(8,128)S(1)}, u32[]{:S(2)}, u32[]{:S(2)}) collective-permute-start(f32[512,512]{1,0:T(8,128)S(1)} %pad_maximum_fusion.1), channel_id=1, source_target_pairs={{0,4},{2,6},{4,0},{6,2},{8,12},{10,14},{12,8},{14,10},{16,20},{18,... | collective-permute-start | bytes 3145736 | tf_op jit(solution)/shard_map/ppermute | solution.py:31
  61.3 23.0 %collective-permute-start.14 = (f32[3,64,512]{2,1,0:T(8,128)S(1)}, f32[3,64,512]{2,1,0:T(8,128)S(1)}, u32[]{:S(2)}, u32[]{:S(2)}) collective-permute-start(f32[3,64,512]{2,1,0:T(8,128)S(1)} %copy-done.33), channel_id=1, source_target_pairs={{0,8},{2,10},{4,12},{6,14},{8,0},{10,2},{12,4},{14,6},{16,24},{18,... | collective-permute-start | bytes 1179656 | tf_op jit(solution)/shard_map/ppermute | solution.py:31
  61.3 23.0 %collective-permute-start.11 = (f32[256,512]{1,0:T(8,128)S(1)}, f32[256,512]{1,0:T(8,128)S(1)}, u32[]{:S(2)}, u32[]{:S(2)}) collective-permute-start(f32[256,512]{1,0:T(8,128)S(1)} %slice.200.refs_10_), channel_id=1, source_target_pairs={{0,1},{1,0},{2,3},{3,2},{4,5},{5,4},{6,7},{7,6},{8,9},{9,8},{10,11... | collective-permute-start | bytes 1572872 | tf_op jit(solution)/shard_map/ppermute | solution.py:31
  62.1 27.0 %collective-permute-start.10 = (f32[2,3,64,384]{3,2,1,0:T(8,128)S(1)}, f32[2,3,64,384]{3,2,1,0:T(8,128)S(1)}, u32[]{:S(2)}, u32[]{:S(2)}) collective-permute-start(f32[2,3,64,384]{3,2,1,0:T(8,128)S(1)} %pad_maximum_fusion.7), channel_id=1, source_target_pairs={{0,16},{2,18},{4,20},{6,22},{8,24},{10,26},{12,28},{14,30},{16,0},... | collective-permute-start | bytes 1769480 | tf_op jit(solution)/shard_map/ppermute | solution.py:31
  91.8 17.4 %collective-permute-start.18 = (f32[4,3,64,512]{3,2,1,0:T(8,128)S(1)}, f32[4,3,64,512]{3,2,1,0:T(8,128)S(1)}, u32[]{:S(2)}, u32[]{:S(2)}) collective-permute-start(f32[4,3,64,512]{3,2,1,0:T(8,128)S(1)} %bitcast.218), channel_id=1, source_target_pairs={{0,2},{2,0},{4,6},{6,4},{8,10},{10,8},{12,14},{14,12},{16,18},{18,... | collective-permute-start | bytes 4718600 | tf_op jit(solution)/shard_map/ppermute | solution.py:31
  91.9 17.3 %collective-permute-start.16 = (f32[256,512]{1,0:T(8,128)S(1)}, f32[256,512]{1,0:T(8,128)S(1)}, u32[]{:S(2)}, u32[]{:S(2)}) collective-permute-start(f32[256,512]{1,0:T(8,128)S(1)} %get-tuple-element.376.refs_14_), channel_id=1, source_target_pairs={{0,1},{1,0},{2,3},{3,2},{4,5},{5,4},{6,7},{7,6},{8,9},{9,8},{10,11... | collective-permute-start | bytes 1572872 | tf_op jit(solution)/shard_map/ppermute | solution.py:31
  93.4 15.7 %collective-permute-start.17 = (f32[256,512]{1,0:T(8,128)}, f32[256,512]{1,0:T(8,128)S(1)}, u32[]{:S(2)}, u32[]{:S(2)}) collective-permute-start(f32[256,512]{1,0:T(8,128)} %collective-permute-done.8.refs_5_), channel_id=1, source_target_pairs={{0,4},{2,6},{4,0},{6,2},{8,12},{10,14},{12,8},{14,10},{16,20},{18,... | collective-permute-start | bytes 1572872 | tf_op jit(solution)/shard_map/ppermute | solution.py:31
  93.9 15.2 %collective-permute-start.15 = (f32[2,3,64,256]{3,2,1,0:T(8,128)S(1)}, f32[2,3,64,256]{3,2,1,0:T(8,128)S(1)}, u32[]{:S(2)}, u32[]{:S(2)}) collective-permute-start(f32[2,3,64,256]{3,2,1,0:T(8,128)S(1)} %slice.158), channel_id=1, source_target_pairs={{0,8},{2,10},{4,12},{6,14},{8,0},{10,2},{12,4},{14,6},{16,24},{18,... | collective-permute-start | bytes 1179656 | tf_op jit(solution)/shard_map/ppermute | solution.py:31
  94.0 12.9 %collective-permute-start.19 = (f32[2,3,64,128]{3,2,1,0:T(8,128)S(1)}, f32[2,3,64,128]{3,2,1,0:T(8,128)S(1)}, u32[]{:S(2)}, u32[]{:S(2)}) collective-permute-start(f32[2,3,64,128]{3,2,1,0:T(8,128)S(1)} %pad_maximum_fusion.20), channel_id=1, source_target_pairs={{0,16},{2,18},{4,20},{6,22},{8,24},{10,26},{12,28},{14,30},{16,0},... | collective-permute-start | bytes 589832 | tf_op jit(solution)/shard_map/ppermute | solution.py:31
  128.1 12.9 %collective-permute-start.24 = (f32[4,3,64,256]{3,2,1,0:T(8,128)S(1)}, f32[4,3,64,256]{3,2,1,0:T(8,128)S(1)}, u32[]{:S(2)}, u32[]{:S(2)}) collective-permute-start(f32[4,3,64,256]{3,2,1,0:T(8,128)S(1)} %bitcast.223), channel_id=1, source_target_pairs={{0,2},{2,0},{4,6},{6,4},{8,10},{10,8},{12,14},{14,12},{16,18},{18,... | collective-permute-start | bytes 2359304 | tf_op jit(solution)/shard_map/ppermute | solution.py:31
  143.2 13.5 %collective-permute-start.26 = (f32[2,64,256]{2,1,0:T(8,128)S(1)}, f32[2,64,256]{2,1,0:T(8,128)S(1)}, u32[]{:S(2)}, u32[]{:S(2)}) collective-permute-start(f32[2,64,256]{2,1,0:T(8,128)S(1)} %get-tuple-element.330), channel_id=1, source_target_pairs={{0,16},{2,18},{4,20},{6,22},{8,24},{10,26},{12,28},{14,30},{16,0},... | collective-permute-start | bytes 393224 | tf_op jit(solution)/shard_map/ppermute | solution.py:31
  158.8 14.0 %collective-permute-start.29 = (f32[2,64,256]{2,1,0:T(8,128)S(1)}, f32[2,64,256]{2,1,0:T(8,128)S(1)}, u32[]{:S(2)}, u32[]{:S(2)}) collective-permute-start(f32[2,64,256]{2,1,0:T(8,128)S(1)} %get-tuple-element.357), channel_id=1, source_target_pairs={{0,4},{2,6},{4,0},{6,2},{8,12},{10,14},{12,8},{14,10},{16,20},{18,... | collective-permute-start | bytes 393224 | tf_op jit(solution)/shard_map/ppermute | solution.py:31
  160.3 12.5 %collective-permute-start.30 = (f32[2,64,256]{2,1,0:T(8,128)S(1)}, f32[2,64,256]{2,1,0:T(8,128)S(1)}, u32[]{:S(2)}, u32[]{:S(2)}) collective-permute-start(f32[2,64,256]{2,1,0:T(8,128)S(1)} %get-tuple-element.359), channel_id=1, source_target_pairs={{0,16},{2,18},{4,20},{6,22},{8,24},{10,26},{12,28},{14,30},{16,0},... | collective-permute-start | bytes 393224 | tf_op jit(solution)/shard_map/ppermute | solution.py:31
  (50 other events, 386.9 us)
where the time goes:
time: 206 us; the launch traced here: 205 us
  waiting for transfers between devices  103 us (50%)
  Pallas kernels  41.2 us (20%)
  starting transfers between devices  40.1 us (19%)
  other arithmetic  10.8 us (5%)
  local copies, waits for them, and re-layouts  7.92 us (4%)
    ppermute x39, waiting for transfers between devices, swap(): return lax.ppermute(array, self.axis, self.pairs)  103 us
    pallas_call x4, Pallas kernels, grads_of(): pl.pallas_call(functools.partial(chunk_kernel, starts, width), out_shape=...  41.2 us
    ppermute x39, starting transfers between devices, swap(): return lax.ppermute(array, self.axis, self.pairs)  40.1 us
  transfers between devices with their start and end apart: 39, of which 20 were waited for; matrix products, arithmetic and copies ran while one was open for 4% of the time, Pallas kernels for 20%

commit v1 on v0

--- a/solution.py
+++ b/solution.py
@@ -62,10 +62,13 @@
 
 def chunk_kernel(starts, width, mine_ref, *refs):
     sources, (keep_ref, send_ref) = refs[:20], refs[20:22]
-    held, piece, up_high, up_low, down_high, down_low, total, done = refs[22:]
+    held, piece, up_high, up_low, down_high, down_low = refs[22:28]
+    high_rows, low_rows, high_grads, low_grads, total, done = refs[28:]
     side, core, far = mine_ref[0], mine_ref[1], mine_ref[2]
     _, blocks, _, depth, _ = piece.shape
-    half = held.shape[2]
+    tokens, half = held.shape[1:]
+    units = keep_ref.shape[0]
+    unit = width // units
 
     copies = []
     for i, start in enumerate(starts):
@@ -96,34 +99,43 @@
     for b in range(4):
         for copy in copies[4 + 4 * b : 8 + 4 * b]:
             copy.wait()
+        here = slice(b * tokens, (b + 1) * tokens)
         pieces = [parts_of(held[2 * b + h]) for h in range(2)]
+        for h in range(2):
+            high_rows[h, here], low_rows[h, here] = pieces[h]
         sums = sum(product(pieces[h], (up_high[at[h], :], up_low[at[h], :]), 1) for h in range(2))
         back = sum(
-            product(
-                parts_of(held[8 + 2 * b + h]), (down_high[at[h], :], down_low[at[h], :]), 1
-            )
+            product(parts_of(held[8 + 2 * b + h]), (down_high[at[h], :], down_low[at[h], :]), 1)
             for h in range(2)
         )
         gate, lift = sums[:, :width], sums[:, width:]
         sigmoid = 1.0 / (1.0 + jnp.exp(-gate))
         back = back * sigmoid
-        grads = parts_of(
-            jnp.concatenate([back * lift * (1.0 + gate * (1.0 - sigmoid)), back * gate], 1)
-        )
-        for h in range(2):
-            term = product(grads, pieces[h], 0)
-            total[h] = term if b == 0 else total[h] + term
+        gate, lift = back * lift * (1.0 + gate * (1.0 - sigmoid)), back * gate
+        grads = [x[:, u * unit : (u + 1) * unit] for u in range(units) for x in (gate, lift)]
+        high_grads[here], low_grads[here] = parts_of(jnp.concatenate(grads, 1))
+        if b % 2 == 1:
+            pair = slice((b - 1) * tokens, (b + 1) * tokens)
+            for h in range(2):
+                term = product(
+                    (high_rows[h, pair], low_rows[h, pair]),
+                    (high_grads[pair], low_grads[pair]),
+                    0,
+                )
+                total[h] = term if b == 1 else total[h] + term
 
     for h, place in ((0, side), (1, 1 - side)):
-        turned = total[h].T
-        for bit in range(2):
-            for ref, whose in ((keep_ref, bit), (send_ref, 1 - bit)):
-
-                @pl.when(core == whose)
-                def _():
-                    for block in range(blocks):
-                        start = (block * 2 + bit) * depth
-                        ref[place * blocks + block] = turned[start : start + depth, :]
+        for u in range(units):
+            for bit in range(2):
+                for ref, whose in ((keep_ref, bit), (send_ref, 1 - bit)):
+
+                    @pl.when(core == whose)
+                    def _():
+                        for block in range(blocks):
+                            start = (block * 2 + bit) * depth
+                            ref[u, place * blocks + block] = total[
+                                h, start : start + depth, u * 2 * unit : (u + 1) * 2 * unit
+                            ]
 
 
 def after(tree):
@@ -156,7 +168,8 @@
         chunks = CHUNKS if part % (CHUNKS * 128) == 0 else 1
         width = part // chunks
         both = 2 * width
-        half = (chunks + 1) // 2 * width
+        sizes = [chunks // 2] + [1] * (chunks // 2) if chunks % 2 == 0 else [chunks]
+        half = sizes[0] * width
         most = (chunks - chunks // 4) * width
         for bit in features[:-1]:
             inputs = bit.joined(inputs, bit.swap(inputs), 1)
@@ -187,6 +200,11 @@
             return blocks[0].reshape((-1,) + blocks[0].shape[-3:])
 
         tokens = inputs.shape[0]
+
+        pairs = [(i, i ^ (1 << (n_bits - 1)) ^ 2) for i in range(n_dp)]
+
+        def diagonal(array):
+            return lax.ppermute(array, "dp", pairs)
 
         oo = columns_of(far.mine, near.mine)
         ox = columns_of(far.mine, 1 - near.mine)
@@ -263,81 +281,96 @@
         ]
         mine = jnp.stack([side.mine, core.mine, far.mine]).astype(jnp.int32)
 
-        def grads_of(ahead, kept_at, come_at, *arrays):
+        def grads_of(ahead, units, kept_at, come_at, *arrays):
+            held = units * width
             feature_rows = n_dp * depth
-            out = jax.ShapeDtypeStruct((n_dp // 2, depth, both), jnp.float32)
+            out = jax.ShapeDtypeStruct((units, n_dp // 2, depth, both), jnp.float32)
             vmem = pl.BlockSpec(memory_space=pltpu.VMEM)
             any_space = pl.BlockSpec(memory_space=pl.ANY)
-            starts = (kept_at, kept_at, come_at, come_at)
+            all_tokens = 4 * tokens
             keep, send = pl.pallas_call(
-                functools.partial(chunk_kernel, starts, width),
+                functools.partial(chunk_kernel, (kept_at, kept_at, come_at, come_at), held),
                 out_shape=(out, out),
                 in_specs=[pl.BlockSpec(memory_space=pltpu.SMEM)] + [any_space] * len(arrays),
                 out_specs=(vmem, vmem),
                 scratch_shapes=[
                     pltpu.VMEM((16,) + inputs.shape, jnp.float32),
-                    pltpu.VMEM((4, n_dp // 4, 3, depth, width), jnp.float32),
-                    pltpu.VMEM((feature_rows, both), jnp.bfloat16),
-                    pltpu.VMEM((feature_rows, both), jnp.bfloat16),
-                    pltpu.VMEM((feature_rows, width), jnp.bfloat16),
-                    pltpu.VMEM((feature_rows, width), jnp.bfloat16),
-                    pltpu.VMEM((2, both, feature_rows // 2), jnp.float32),
+                    pltpu.VMEM((4, n_dp // 4, 3, depth, held), jnp.float32),
+                    pltpu.VMEM((feature_rows, 2 * held), jnp.bfloat16),
+                    pltpu.VMEM((feature_rows, 2 * held), jnp.bfloat16),
+                    pltpu.VMEM((feature_rows, held), jnp.bfloat16),
+                    pltpu.VMEM((feature_rows, held), jnp.bfloat16),
+                    pltpu.VMEM((2, all_tokens, feature_rows // 2), jnp.bfloat16),
+                    pltpu.VMEM((2, all_tokens, feature_rows // 2), jnp.bfloat16),
+                    pltpu.VMEM((all_tokens, 2 * held), jnp.bfloat16),
+                    pltpu.VMEM((all_tokens, 2 * held), jnp.bfloat16),
+                    pltpu.VMEM((2, feature_rows // 2, 2 * held), jnp.float32),
                     pltpu.SemaphoreType.DMA((20,)),
                 ],
                 compiler_params=pltpu.CompilerParams(vmem_limit_bytes=VMEM_LIMIT),
                 cost_estimate=pl.CostEstimate(
-                    flops=24 * tokens * feature_rows * 5 * width // 2,
-                    bytes_accessed=16 * tokens * feature_rows,
-                    transcendentals=4 * tokens * width,
+                    flops=30 * all_tokens * feature_rows * held,
+                    bytes_accessed=8 * all_tokens * feature_rows,
+                    transcendentals=all_tokens * held,
                 ),
             )(mine, *arrays)
-            shape = [2] * (n_bits - 1) + [depth, both]
+            shape = [units] + [2] * (n_bits - 1) + [depth, both]
             send, ahead = after((send, ahead))
-            return (keep.reshape(shape), core.swap(send).reshape(shape)), ahead
+            return [keep.reshape(shape), core.swap(send).reshape(shape)], ahead
 
         kept, kept_core = s["kept"], s["kept_core"]
-        arrived = {0: (s["come"], s["come_core"])}
+        arrived = (s["come"], s["come_core"])
         late = s["late"]
+        calls = len(sizes)
+        firsts = [sum(sizes[:call]) for call in range(calls)]
         stages = {}
-        fresh = None
-        for step in range(chunks + 4):
+        for step in range(calls + 2):
             new = {}
-            if step - 3 >= 0 and step - 3 < chunks:
-                keep, send = stages[step - 3]
-                new[step - 3] = near.ordered(keep, near.swap(send), 0)
-            if step - 2 >= 0 and step - 2 < chunks:
-                keep, send = stages[step - 2]
-                grad = far.ordered(keep, far.swap(send), 1)
-                new[step - 2] = (near.own(grad, 0), near.other(grad, 0))
-            if step - 1 >= 0 and step - 1 < chunks:
-                terms = stages[step - 1]
-                for bit in middle:
-                    keep, send = (sum(part(x, 1) for x in terms) for part in (bit.own, bit.other))
-                    terms = (keep, bit.swap(send))
-                grad = sum(terms)
-                new[step - 1] = (far.own(grad, 0), far.other(grad, 0))
-            if step == 0 and half < part:
-                fresh = over_middle([jnp.concatenate(late, -1) if most < part else late])
-            if step == 1 and half < part:
-                fresh = arranged([[p[0][0], p[0][1]] for p in fresh])
-                fresh = (fresh, core.swap(fresh))
-            if step < chunks:
-                group, start = (0, step * width) if step * width < half else (1, step * width - half)
-                new[step], fresh = grads_of(
-                    fresh, step * width, start, *tokens_of, kept, kept_core, *arrived[group]
+            for call in range(calls):
+                if step == call + 2:
+                    own, beside, beyond, across = stages[call]
+                    own = near.ordered(own, near.swap(beside), 1)
+                    beyond = near.ordered(far.swap(beyond), diagonal(across), 1)
+                    new[call] = far.ordered(own, beyond, 2)
+                if step == call + 1:
+                    terms = stages[call]
+                    for bit in middle:
+                        keep, send = (
+                            sum(part(x, 2) for x in terms) for part in (bit.own, bit.other)
+                        )
+                        terms = [keep, bit.swap(send)]
+                    new[call] = [
+                        sum(there(here(x, 1), 1) for x in terms)
+                        for here in (far.own, far.other)
+                        for there in (near.own, near.other)
+                    ]
+            if step < calls:
+                fresh = None
+                if step == 0 and calls > 1:
+                    fresh = over_middle([jnp.concatenate(late, -1) if most < part else late])
+                come_at = max(firsts[step] * width - half, 0)
+                terms, (fresh, new) = grads_of(
+                    (fresh, new), sizes[step], firsts[step] * width, come_at,
+                    *tokens_of, kept, kept_core, *arrived,
                 )
+                new[step] = terms
+                if step == 0 and calls > 1:
+                    fresh = arranged([[p[0][0], p[0][1]] for p in fresh])
+                    arrived = (fresh, core.swap(fresh))
             stages.update(new)
-            if step < chunks + 3:
-                stages, kept, kept_core, tokens_of, fresh, arrived = after(
-                    (stages, kept, kept_core, tokens_of, fresh, arrived)
+            if step < calls + 1:
+                stages, kept, kept_core, tokens_of, arrived = after(
+                    (stages, kept, kept_core, tokens_of, arrived)
                 )
-            if step == 1 and half < part:
-                arrived[1] = fresh
+
+        pieces = []
+        for call in range(calls):
+            pieces += [stages[call][u] for u in range(sizes[call])]
 
         def assembled(which):
             return jnp.concatenate(
                 [
-                    stages[chunk][n, f, :, which * width : (which + 1) * width]
+                    pieces[chunk][n, f, :, which * width : (which + 1) * width]
                     for f in range(2)
                     for n in range(2)
                     for chunk in range(chunks)

time: 206 us -> 197 us (0.956)
  Pallas kernels: 41.2 us -> 34.9 us
    ppermute x39 -> x35, waiting for transfers between devices: 103 us -> 94.1 us  [swap(): return lax.ppermute(array, self.axis, self.pairs)]
    ppermute x0 -> x3, waiting for transfers between devices: none -> 6.61 us  [diagonal(): return lax.ppermute(array, 'dp', pairs)]
    pallas_call x4 -> x3, Pallas kernels: 41.2 us -> 34.9 us  [grads_of(): pl.pallas_call(functools.partial(chunk_kernel, (kept_at, kept_at, come_at...]
    ppermute x39 -> x35, starting transfers between devices: 40.1 us -> 34 us  [swap(): return lax.ppermute(array, self.axis, self.pairs)]
    ppermute x0 -> x3, starting transfers between devices: none -> 5.69 us  [diagonal(): return lax.ppermute(array, 'dp', pairs)]
    unnamed x84 -> x70, local copies, waits for them, and re-layouts: 3.29 us -> 6.35 us
  transfers between devices with their start and end apart: 39 -> 38, of which waited for: 20 -> 18; matrix products, arithmetic and copies ran while one was open for 4% -> 3% of each run, Pallas kernels for 20% -> 18%
where the time goes in v1:
time: 197 us; the launch traced here: 196 us
  waiting for transfers between devices  101 us (51%)
  starting transfers between devices  39.6 us (20%)
  Pallas kernels  34.9 us (18%)
  other arithmetic  10.7 us (5%)
  local copies, waits for them, and re-layouts  8.85 us (4%)
    ppermute x35, waiting for transfers between devices, swap(): return lax.ppermute(array, self.axis, self.pairs)  94.1 us
    pallas_call x3, Pallas kernels, grads_of(): pl.pallas_call(functools.partial(chunk_kernel, (kept_at, kept_at, come_at...  34.9 us
    ppermute x35, starting transfers between devices, swap(): return lax.ppermute(array, self.axis, self.pairs)  34 us
    ppermute x3, waiting for transfers between devices, diagonal(): return lax.ppermute(array, 'dp', pairs)  6.61 us
    unnamed x70, local copies, waits for them, and re-layouts  6.35 us
    ppermute x3, starting transfers between devices, diagonal(): return lax.ppermute(array, 'dp', pairs)  5.69 us
  transfers between devices with their start and end apart: 38, of which 18 were waited for; matrix products, arithmetic and copies ran while one was open for 3% of the time, Pallas kernels for 18%

profile of v1, /device:TPU:0, one launch (start us, length us, event | category | flops | bytes accessed | tf_op | source)
XLA Modules:
  0.0 196.4 jit_solution(5253381944467132137)
XLA Ops:
  0.6 4.1 %collective-permute-start.1 = (f32[256,512]{1,0:T(8,128)}, f32[256,512]{1,0:T(8,128)}, u32[]{:S(2)}, u32[]{:S(2)}) collective-permute-start(f32[256,512]{1,0:T(8,128)} %refs_0_.2), channel_id=1, source_target_pairs={{0,16},{2,18},{4,20},{6,22},{8,24},{10,26},{12,28},{14,30},{16,0},... | collective-permute-start | bytes 1572872 | tf_op jit(solution)/shard_map/ppermute | solution.py:31
  10.4 16.4 %collective-permute-done.4 = f32[3,64,512]{2,1,0:T(8,128)} collective-permute-done((f32[3,64,512]{2,1,0:T(8,128)S(1)}, f32[3,64,512]{2,1,0:T(8,128)}, u32[]{:S(2)}, u32[]{:S(2)}) %collective-permute-start.4) | collective-permute-done | bytes 393248 | tf_op jit(solution)/shard_map/ppermute | solution.py:31
  26.9 3.9 %collective-permute-done.refs_9_ = f32[256,512]{1,0:T(8,128)S(1)} collective-permute-done((f32[256,512]{1,0:T(8,128)}, f32[256,512]{1,0:T(8,128)S(1)}, u32[]{:S(2)}, u32[]{:S(2)}) %collective-permute-start) | collective-permute-done | bytes 524320 | tf_op jit(solution)/shard_map/ppermute | solution.py:31
  38.0 16.1 %collective-permute-done.6 = f32[448,512]{1,0:T(8,128)S(1)} collective-permute-done((f32[448,512]{1,0:T(8,128)S(1)}, f32[448,512]{1,0:T(8,128)S(1)}, u32[]{:S(2)}, u32[]{:S(2)}) %collective-permute-start.6) | collective-permute-done | bytes 917536 | tf_op jit(solution)/shard_map/ppermute | solution.py:31
  54.3 4.2 %collective-permute-done.5.refs_12_ = f32[256,512]{1,0:T(8,128)} collective-permute-done((f32[256,512]{1,0:T(8,128)}, f32[256,512]{1,0:T(8,128)}, u32[]{:S(2)}, u32[]{:S(2)}) %collective-permute-start.5) | collective-permute-done | bytes 524320 | tf_op jit(solution)/shard_map/ppermute | solution.py:31
  62.9 2.0 collective-permute-start.10
  66.9 18.3 %collective-permute-done.12 = f32[512,512]{1,0:T(8,128)S(1)} collective-permute-done((f32[512,512]{1,0:T(8,128)S(1)}, f32[512,512]{1,0:T(8,128)S(1)}, u32[]{:S(2)}, u32[]{:S(2)}) %collective-permute-start.12) | collective-permute-done | bytes 1048608 | tf_op jit(solution)/shard_map/ppermute | solution.py:31
  86.1 3.9 %collective-permute-done.10 = f32[2,3,64,384]{3,2,1,0:T(8,128)S(1)} collective-permute-done((f32[2,3,64,384]{3,2,1,0:T(8,128)S(1)}, f32[2,3,64,384]{3,2,1,0:T(8,128)S(1)}, u32[]{:S(2)}, u32[]{:S(2)}) %collective-permute-start.10) | collective-permute-done | bytes 589856 | tf_op jit(solution)/shard_map/ppermute | solution.py:31
  93.4 1.7 collective-permute-start.19
  95.1 11.2 %collective-permute-done.19 = f32[2,3,64,128]{3,2,1,0:T(8,128)S(1)} collective-permute-done((f32[2,3,64,128]{3,2,1,0:T(8,128)S(1)}, f32[2,3,64,128]{3,2,1,0:T(8,128)S(1)}, u32[]{:S(2)}, u32[]{:S(2)}) %collective-permute-start.19) | collective-permute-done | bytes 196640 | tf_op jit(solution)/shard_map/ppermute | solution.py:31
  106.3 2.2 %collective-permute-done.15 = f32[2,3,64,256]{3,2,1,0:T(8,128)S(1)} collective-permute-done((f32[2,3,64,256]{3,2,1,0:T(8,128)S(1)}, f32[2,3,64,256]{3,2,1,0:T(8,128)S(1)}, u32[]{:S(2)}, u32[]{:S(2)}) %collective-permute-start.15) | collective-permute-done | bytes 393248 | tf_op jit(solution)/shard_map/ppermute | solution.py:31
  114.7 15.4 %shard_map.136 = (f32[2,8,64,256]{3,2,1,0:T(8,128)}, f32[2,8,64,256]{3,2,1,0:T(8,128)}) custom-call(s32[3]{0:T(128)} %pad_add_fusion.mine_ref, f32[256,512]{1,0:T(8,128)} %refs_0_.2, f32[256,512]{1,0:T(8,128)} %copy-done.19, f32[256,512]{1,0:T(8,128)} %collective-permute-done.2.refs_2_, f32[256,512]{1,0:T(8,128)} %collective-permute-done.7.refs_3_, ...), custom_call_target="tpu_custom_call" | custom-call | flops 8053063680 | bytes 8388608 | tf_op jit(solution)/shard_map/pallas_call | solution.py:291
  131.0 3.2 %collective-permute-done.23.refs_19_ = f32[4,3,64,256]{3,2,1,0:T(8,128)} collective-permute-done((f32[4,3,64,256]{3,2,1,0:T(8,128)S(1)}, f32[4,3,64,256]{3,2,1,0:T(8,128)}, u32[]{:S(2)}, u32[]{:S(2)}) %collective-permute-start.23) | collective-permute-done | bytes 786464 | tf_op jit(solution)/shard_map/ppermute | solution.py:31
  136.4 9.9 %shard_map.137 = (f32[1,8,64,256]{3,2,1,0:T(8,128)}, f32[1,8,64,256]{3,2,1,0:T(8,128)}) custom-call(s32[3]{0:T(128)} %pad_add_fusion.mine_ref, f32[256,512]{1,0:T(8,128)} %refs_0_.2, f32[256,512]{1,0:T(8,128)} %copy-done.19, f32[256,512]{1,0:T(8,128)} %collective-permute-done.2.refs_2_, f32[256,512]{1,0:T(8,128)} %collective-permute-done.7.refs_3_, ...), custom_call_target="tpu_custom_call" | custom-call | flops 4026531840 | bytes 8388608 | tf_op jit(solution)/shard_map/pallas_call | solution.py:291
  146.3 3.1 %collective-permute-done.24 = f32[2,2,2,64,256]{4,3,0,2,1:T(8,128)} collective-permute-done((f32[2,2,2,64,256]{4,3,0,2,1:T(8,128)}, f32[2,2,2,64,256]{4,3,0,2,1:T(8,128)}, u32[]{:S(2)}, u32[]{:S(2)}) %collective-permute-start.24) | collective-permute-done | bytes 524320 | tf_op jit(solution)/shard_map/ppermute | solution.py:31
  150.7 1.9 collective-permute-done.25
  156.2 2.1 %collective-permute-start.28 = (f32[2,64,256]{2,1,0:T(8,128)S(1)}, f32[2,64,256]{2,1,0:T(8,128)S(1)}, u32[]{:S(2)}, u32[]{:S(2)}) collective-permute-start(f32[2,64,256]{2,1,0:T(8,128)S(1)} %get-tuple-element.323), channel_id=1, source_target_pairs={{0,20},{2,22},{4,16},{6,18},{8,28},{10,30},{12,24},{14,26},{16,4},... | collective-permute-start | bytes 393224 | tf_op jit(solution)/shard_map/ppermute | solution.py:207
  158.3 9.6 %shard_map.138 = (f32[1,8,64,256]{3,2,1,0:T(8,128)}, f32[1,8,64,256]{3,2,1,0:T(8,128)}) custom-call(s32[3]{0:T(128)} %pad_add_fusion.mine_ref, f32[256,512]{1,0:T(8,128)} %refs_0_.2, f32[256,512]{1,0:T(8,128)} %copy-done.19, f32[256,512]{1,0:T(8,128)} %collective-permute-done.2.refs_2_, f32[256,512]{1,0:T(8,128)} %collective-permute-done.7.refs_3_, ...), custom_call_target="tpu_custom_call" | custom-call | flops 4026531840 | bytes 8388608 | tf_op jit(solution)/shard_map/pallas_call | solution.py:291
  170.8 1.9 collective-permute-done.30
  174.0 2.0 %collective-permute-start.32 = (f32[1,64,256]{2,1,0:T(8,128)S(1)}, f32[1,64,256]{2,1,0:T(8,128)S(1)}, u32[]{:S(2)}, u32[]{:S(2)}) collective-permute-start(f32[1,64,256]{2,1,0:T(8,128)S(1)} %get-tuple-element.336), channel_id=1, source_target_pairs={{0,16},{2,18},{4,20},{6,22},{8,24},{10,26},{12,28},{14,30},{16,0},... | collective-permute-start | bytes 196616 | tf_op jit(solution)/shard_map/ppermute | solution.py:31
  177.3 3.5 %collective-permute-done.32 = f32[1,64,256]{2,1,0:T(8,128)S(1)} collective-permute-done((f32[1,64,256]{2,1,0:T(8,128)S(1)}, f32[1,64,256]{2,1,0:T(8,128)S(1)}, u32[]{:S(2)}, u32[]{:S(2)}) %collective-permute-start.32) | collective-permute-done | bytes 65568 | tf_op jit(solution)/shard_map/ppermute | solution.py:31
  180.9 3.8 %collective-permute-done.33 = f32[1,64,256]{2,1,0:T(8,128)S(1)} collective-permute-done((f32[1,64,256]{2,1,0:T(8,128)S(1)}, f32[1,64,256]{2,1,0:T(8,128)S(1)}, u32[]{:S(2)}, u32[]{:S(2)}) %collective-permute-start.33) | collective-permute-done | bytes 65568 | tf_op jit(solution)/shard_map/ppermute | solution.py:207
  186.9 2.4 %collective-permute-start.37 = (f32[1,64,256]{2,1,0:T(8,128)S(1)}, f32[1,64,256]{2,1,0:T(8,128)S(1)}, u32[]{:S(2)}, u32[]{:S(2)}) collective-permute-start(f32[1,64,256]{2,1,0:T(8,128)S(1)} %get-tuple-element.345), channel_id=1, source_target_pairs={{0,20},{2,22},{4,16},{6,18},{8,28},{10,30},{12,24},{14,26},{16,4},... | collective-permute-start | bytes 196616 | tf_op jit(solution)/shard_map/ppermute | solution.py:207
  189.4 2.6 %collective-permute-done.36 = f32[1,64,256]{2,1,0:T(8,128)S(1)} collective-permute-done((f32[1,64,256]{2,1,0:T(8,128)S(1)}, f32[1,64,256]{2,1,0:T(8,128)S(1)}, u32[]{:S(2)}, u32[]{:S(2)}) %collective-permute-start.36) | collective-permute-done | bytes 65568 | tf_op jit(solution)/shard_map/ppermute | solution.py:31
  (184 shorter events, 49.4 us)
Async XLA Ops:
  0.6 30.2 %collective-permute-start.1 = (f32[256,512]{1,0:T(8,128)}, f32[256,512]{1,0:T(8,128)}, u32[]{:S(2)}, u32[]{:S(2)}) collective-permute-start(f32[256,512]{1,0:T(8,128)} %refs_0_.2), channel_id=1, source_target_pairs={{0,16},{2,18},{4,20},{6,22},{8,24},{10,26},{12,28},{14,30},{16,0},... | collective-permute-start | bytes 1572872 | tf_op jit(solution)/shard_map/ppermute | solution.py:31
  4.7 26.1 %collective-permute-start.2 = (f32[256,512]{1,0:T(8,128)}, f32[256,512]{1,0:T(8,128)}, u32[]{:S(2)}, u32[]{:S(2)}) collective-permute-start(f32[256,512]{1,0:T(8,128)} %refs_0_.2), channel_id=1, source_target_pairs={{0,4},{2,6},{4,0},{6,2},{8,12},{10,14},{12,8},{14,10},{16,20},{18,... | collective-permute-start | bytes 1572872 | tf_op jit(solution)/shard_map/ppermute | solution.py:31
  6.3 24.6 %collective-permute-start.3 = (f32[256,512]{1,0:T(8,128)}, f32[256,512]{1,0:T(8,128)S(1)}, u32[]{:S(2)}, u32[]{:S(2)}) collective-permute-start(f32[256,512]{1,0:T(8,128)} %refs_0_.2), channel_id=1, source_target_pairs={{0,1},{1,0},{2,3},{3,2},{4,5},{5,4},{6,7},{7,6},{8,9},{9,8},{10,11... | collective-permute-start | bytes 1572872 | tf_op jit(solution)/shard_map/ppermute | solution.py:31
  7.8 23.1 %collective-permute-start = (f32[256,512]{1,0:T(8,128)}, f32[256,512]{1,0:T(8,128)S(1)}, u32[]{:S(2)}, u32[]{:S(2)}) collective-permute-start(f32[256,512]{1,0:T(8,128)} %refs_8_.2), channel_id=1, source_target_pairs={{0,1},{1,0},{2,3},{3,2},{4,5},{5,4},{6,7},{7,6},{8,9},{9,8},{10,11... | collective-permute-start | bytes 1572872 | tf_op jit(solution)/shard_map/ppermute | solution.py:31
  9.7 17.1 %collective-permute-start.4 = (f32[3,64,512]{2,1,0:T(8,128)S(1)}, f32[3,64,512]{2,1,0:T(8,128)}, u32[]{:S(2)}, u32[]{:S(2)}) collective-permute-start(f32[3,64,512]{2,1,0:T(8,128)S(1)} %pad_maximum_fusion.10), channel_id=1, source_target_pairs={{0,4},{2,6},{4,0},{6,2},{8,12},{10,14},{12,8},{14,10},{16,20},{18,... | collective-permute-start | bytes 1179656 | tf_op jit(solution)/shard_map/ppermute | solution.py:31
  33.5 20.7 %collective-permute-start.6 = (f32[448,512]{1,0:T(8,128)S(1)}, f32[448,512]{1,0:T(8,128)S(1)}, u32[]{:S(2)}, u32[]{:S(2)}) collective-permute-start(f32[448,512]{1,0:T(8,128)S(1)} %pad_maximum_fusion.2), channel_id=1, source_target_pairs={{0,4},{2,6},{4,0},{6,2},{8,12},{10,14},{12,8},{14,10},{16,20},{18,... | collective-permute-start | bytes 2752520 | tf_op jit(solution)/shard_map/ppermute | solution.py:31
  34.1 24.5 %collective-permute-start.5 = (f32[256,512]{1,0:T(8,128)}, f32[256,512]{1,0:T(8,128)}, u32[]{:S(2)}, u32[]{:S(2)}) collective-permute-start(f32[256,512]{1,0:T(8,128)} %refs_8_.2), channel_id=1, source_target_pairs={{0,16},{2,18},{4,20},{6,22},{8,24},{10,26},{12,28},{14,30},{16,0},... | collective-permute-start | bytes 1572872 | tf_op jit(solution)/shard_map/ppermute | solution.py:31
  34.4 24.1 %collective-permute-start.7 = (f32[256,512]{1,0:T(8,128)}, f32[256,512]{1,0:T(8,128)}, u32[]{:S(2)}, u32[]{:S(2)}) collective-permute-start(f32[256,512]{1,0:T(8,128)} %collective-permute-done.2.refs_2_), channel_id=1, source_target_pairs={{0,1},{1,0},{2,3},{3,2},{4,5},{5,4},{6,7},{7,6},{8,9},{9,8},{10,11... | collective-permute-start | bytes 1572872 | tf_op jit(solution)/shard_map/ppermute | solution.py:31
  35.9 22.6 %collective-permute-start.8 = (f32[256,512]{1,0:T(8,128)}, f32[256,512]{1,0:T(8,128)}, u32[]{:S(2)}, u32[]{:S(2)}) collective-permute-start(f32[256,512]{1,0:T(8,128)} %collective-permute-done.1.refs_4_), channel_id=1, source_target_pairs={{0,1},{1,0},{2,3},{3,2},{4,5},{5,4},{6,7},{7,6},{8,9},{9,8},{10,11... | collective-permute-start | bytes 1572872 | tf_op jit(solution)/shard_map/ppermute | solution.py:31
  36.5 17.8 %collective-permute-start.9 = (f32[3,64,512]{2,1,0:T(8,128)S(1)}, f32[3,64,512]{2,1,0:T(8,128)S(1)}, u32[]{:S(2)}, u32[]{:S(2)}) collective-permute-start(f32[3,64,512]{2,1,0:T(8,128)S(1)} %pad_maximum_fusion.9), channel_id=1, source_target_pairs={{0,8},{2,10},{4,12},{6,14},{8,0},{10,2},{12,4},{14,6},{16,24},{18,... | collective-permute-start | bytes 1179656 | tf_op jit(solution)/shard_map/ppermute | solution.py:31
  58.5 27.5 %collective-permute-start.13 = (f32[256,512]{1,0:T(8,128)}, f32[256,512]{1,0:T(8,128)S(1)}, u32[]{:S(2)}, u32[]{:S(2)}) collective-permute-start(f32[256,512]{1,0:T(8,128)} %collective-permute-done.5.refs_12_), channel_id=1, source_target_pairs={{0,1},{1,0},{2,3},{3,2},{4,5},{5,4},{6,7},{7,6},{8,9},{9,8},{10,11... | collective-permute-start | bytes 1572872 | tf_op jit(solution)/shard_map/ppermute | solution.py:31
  61.3 23.9 %collective-permute-start.12 = (f32[512,512]{1,0:T(8,128)S(1)}, f32[512,512]{1,0:T(8,128)S(1)}, u32[]{:S(2)}, u32[]{:S(2)}) collective-permute-start(f32[512,512]{1,0:T(8,128)S(1)} %pad_maximum_fusion.1), channel_id=1, source_target_pairs={{0,4},{2,6},{4,0},{6,2},{8,12},{10,14},{12,8},{14,10},{16,20},{18,... | collective-permute-start | bytes 3145736 | tf_op jit(solution)/shard_map/ppermute | solution.py:31
  62.9 27.1 %collective-permute-start.10 = (f32[2,3,64,384]{3,2,1,0:T(8,128)S(1)}, f32[2,3,64,384]{3,2,1,0:T(8,128)S(1)}, u32[]{:S(2)}, u32[]{:S(2)}) collective-permute-start(f32[2,3,64,384]{3,2,1,0:T(8,128)S(1)} %pad_maximum_fusion.7), channel_id=1, source_target_pairs={{0,16},{2,18},{4,20},{6,22},{8,24},{10,26},{12,28},{14,30},{16,0},... | collective-permute-start | bytes 1769480 | tf_op jit(solution)/shard_map/ppermute | solution.py:31
  64.9 21.2 %collective-permute-start.11 = (f32[256,512]{1,0:T(8,128)S(1)}, f32[256,512]{1,0:T(8,128)S(1)}, u32[]{:S(2)}, u32[]{:S(2)}) collective-permute-start(f32[256,512]{1,0:T(8,128)S(1)} %slice.208.refs_10_), channel_id=1, source_target_pairs={{0,1},{1,0},{2,3},{3,2},{4,5},{5,4},{6,7},{7,6},{8,9},{9,8},{10,11... | collective-permute-start | bytes 1572872 | tf_op jit(solution)/shard_map/ppermute | solution.py:31
  65.4 20.7 %collective-permute-start.14 = (f32[3,64,512]{2,1,0:T(8,128)}, f32[3,64,512]{2,1,0:T(8,128)S(1)}, u32[]{:S(2)}, u32[]{:S(2)}) collective-permute-start(f32[3,64,512]{2,1,0:T(8,128)} %collective-permute-done.4), channel_id=1, source_target_pairs={{0,8},{2,10},{4,12},{6,14},{8,0},{10,2},{12,4},{14,6},{16,24},{18,... | collective-permute-start | bytes 1179656 | tf_op jit(solution)/shard_map/ppermute | solution.py:31
  91.7 17.6 %collective-permute-start.18 = (f32[4,3,64,512]{3,2,1,0:T(8,128)S(1)}, f32[4,3,64,512]{3,2,1,0:T(8,128)S(1)}, u32[]{:S(2)}, u32[]{:S(2)}) collective-permute-start(f32[4,3,64,512]{3,2,1,0:T(8,128)S(1)} %bitcast.313), channel_id=1, source_target_pairs={{0,2},{2,0},{4,6},{6,4},{8,10},{10,8},{12,14},{14,12},{16,18},{18,... | collective-permute-start | bytes 4718600 | tf_op jit(solution)/shard_map/ppermute | solution.py:31
  91.8 16.7 %collective-permute-start.16 = (f32[256,512]{1,0:T(8,128)S(1)}, f32[256,512]{1,0:T(8,128)S(1)}, u32[]{:S(2)}, u32[]{:S(2)}) collective-permute-start(f32[256,512]{1,0:T(8,128)S(1)} %get-tuple-element.313.refs_14_), channel_id=1, source_target_pairs={{0,1},{1,0},{2,3},{3,2},{4,5},{5,4},{6,7},{7,6},{8,9},{9,8},{10,11... | collective-permute-start | bytes 1572872 | tf_op jit(solution)/shard_map/ppermute | solution.py:31
  92.4 16.1 %collective-permute-start.17 = (f32[256,512]{1,0:T(8,128)}, f32[256,512]{1,0:T(8,128)S(1)}, u32[]{:S(2)}, u32[]{:S(2)}) collective-permute-start(f32[256,512]{1,0:T(8,128)} %collective-permute-done.8.refs_5_), channel_id=1, source_target_pairs={{0,4},{2,6},{4,0},{6,2},{8,12},{10,14},{12,8},{14,10},{16,20},{18,... | collective-permute-start | bytes 1572872 | tf_op jit(solution)/shard_map/ppermute | solution.py:31
  93.3 15.2 %collective-permute-start.15 = (f32[2,3,64,256]{3,2,1,0:T(8,128)S(1)}, f32[2,3,64,256]{3,2,1,0:T(8,128)S(1)}, u32[]{:S(2)}, u32[]{:S(2)}) collective-permute-start(f32[2,3,64,256]{3,2,1,0:T(8,128)S(1)} %slice.164), channel_id=1, source_target_pairs={{0,8},{2,10},{4,12},{6,14},{8,0},{10,2},{12,4},{14,6},{16,24},{18,... | collective-permute-start | bytes 1179656 | tf_op jit(solution)/shard_map/ppermute | solution.py:31
  113.8 16.4 %collective-permute-start.21 = (f32[2,3,64,256]{3,2,1,0:T(8,128)S(1)}, f32[2,3,64,256]{3,2,1,0:T(8,128)S(1)}, u32[]{:S(2)}, u32[]{:S(2)}) collective-permute-start(f32[2,3,64,256]{3,2,1,0:T(8,128)S(1)} %constant_dynamic-update-slice_fusion), channel_id=1, source_target_pairs={{0,8},{2,10},{4,12},{6,14},{8,0},{10,2},{12,4},{14,6},{16,24},{18,... | collective-permute-start | bytes 1179656 | tf_op jit(solution)/shard_map/ppermute | solution.py:31
  135.1 14.3 %collective-permute-start.24 = (f32[2,2,2,64,256]{4,3,0,2,1:T(8,128)}, f32[2,2,2,64,256]{4,3,0,2,1:T(8,128)}, u32[]{:S(2)}, u32[]{:S(2)}) collective-permute-start(f32[2,2,2,64,256]{4,3,0,2,1:T(8,128)} %add_bitcast_fusion), channel_id=1, source_target_pairs={{0,8},{2,10},{4,12},{6,14},{8,0},{10,2},{12,4},{14,6},{16,24},{18,... | collective-permute-start | bytes 1572872 | tf_op jit(solution)/shard_map/ppermute | solution.py:31
  152.6 17.2 %collective-permute-start.29 = (f32[1,2,2,64,256]{4,3,2,1,0:T(8,128)S(1)}, f32[1,2,2,64,256]{4,3,2,1,0:T(8,128)S(1)}, u32[]{:S(2)}, u32[]{:S(2)}) collective-permute-start(f32[1,2,2,64,256]{4,3,2,1,0:T(8,128)S(1)} %add_bitcast_fusion.2), channel_id=1, source_target_pairs={{0,8},{2,10},{4,12},{6,14},{8,0},{10,2},{12,4},{14,6},{16,24},{18,... | collective-permute-start | bytes 786440 | tf_op jit(solution)/shard_map/ppermute | solution.py:31
  153.9 14.0 %collective-permute-start.26 = (f32[2,64,256]{2,1,0:T(8,128)S(1)}, f32[2,64,256]{2,1,0:T(8,128)S(1)}, u32[]{:S(2)}, u32[]{:S(2)}) collective-permute-start(f32[2,64,256]{2,1,0:T(8,128)S(1)} %get-tuple-element.321), channel_id=1, source_target_pairs={{0,4},{2,6},{4,0},{6,2},{8,12},{10,14},{12,8},{14,10},{16,20},{18,... | collective-permute-start | bytes 393224 | tf_op jit(solution)/shard_map/ppermute | solution.py:31
  156.2 13.5 %collective-permute-start.28 = (f32[2,64,256]{2,1,0:T(8,128)S(1)}, f32[2,64,256]{2,1,0:T(8,128)S(1)}, u32[]{:S(2)}, u32[]{:S(2)}) collective-permute-start(f32[2,64,256]{2,1,0:T(8,128)S(1)} %get-tuple-element.323), channel_id=1, source_target_pairs={{0,20},{2,22},{4,16},{6,18},{8,28},{10,30},{12,24},{14,26},{16,4},... | collective-permute-start | bytes 393224 | tf_op jit(solution)/shard_map/ppermute | solution.py:207
  (42 other events, 230.9 us)

commit v2 on v1

--- a/solution.py
+++ b/solution.py
@@ -9,7 +9,7 @@
 
 STEP = 100
 CHUNKS = 4
-VMEM_LIMIT = 60 * 1024 * 1024
+VMEM_LIMIT = 52 * 1024 * 1024
 
 
 def adam_update(weight, first, second, grad):
@@ -77,7 +77,7 @@
     for b in range(4):
         for i in (2 * b, 2 * b + 1, 8 + 2 * b, 9 + 2 * b):
             copies.append(pltpu.make_async_copy(sources[i], held.at[i], done.at[4 + i]))
-    for copy in copies:
+    for copy in copies[:8]:
         copy.start()
 
     for i, (place, bit) in enumerate(
@@ -95,10 +95,14 @@
                     down_high[pl.ds(row, depth), :] = high
                     down_low[pl.ds(row, depth), :] = low
 
+    for copy in copies[8:12]:
+        copy.start()
     at = [pl.ds(pl.multiple_of(h * half, half), half) for h in (side, 1 - side)]
     for b in range(4):
         for copy in copies[4 + 4 * b : 8 + 4 * b]:
             copy.wait()
+        for copy in copies[12 + 4 * b : 16 + 4 * b]:
+            copy.start()
         here = slice(b * tokens, (b + 1) * tokens)
         pieces = [parts_of(held[2 * b + h]) for h in range(2)]
         for h in range(2):
@@ -208,6 +212,8 @@
 
         oo = columns_of(far.mine, near.mine)
         ox = columns_of(far.mine, 1 - near.mine)
+        xx = columns_of(1 - far.mine, 1 - near.mine)
+        n_weight = 3 * depth * part // cotangent.shape[1]
         s = after(
             dict(
                 in_far=far.swap(inputs),
@@ -219,13 +225,11 @@
                 cotangent=cotangent,
                 oo=oo,
                 xo=columns_of(1 - far.mine, near.mine),
-                xx=columns_of(1 - far.mine, 1 - near.mine),
-            )
-        )
-
-        n_weight = 3 * depth * part // cotangent.shape[1]
-        by_near = jnp.concatenate([s["xx"].reshape(n_weight, -1), s["cotangent"]], 0)
-        by_near = near.swap(by_near)
+                by_near=jnp.concatenate([xx.reshape(n_weight, -1), cotangent], 0),
+            )
+        )
+
+        by_near = near.swap(s["by_near"])
         s = after(
             dict(
                 s,

time: 197 us -> 192 us (0.975)
  waiting for transfers between devices: 101 us -> 98.2 us
  Pallas kernels: 34.9 us -> 32.2 us
    unnamed x70 -> x64, local copies, waits for them, and re-layouts: 6.35 us -> 2 us
    pallas_call x3, Pallas kernels: 34.9 us -> 32.2 us  [grads_of(): pl.pallas_call(functools.partial(chunk_kernel, (kept_at, kept_at, come_at...]
    ppermute x35, waiting for transfers between devices: 94.1 us -> 91.7 us  [swap(): return lax.ppermute(array, self.axis, self.pairs)]
  transfers between devices with their start and end apart: 38 -> 38, of which waited for: 18 -> 19; matrix products, arithmetic and copies ran while one was open for 3% -> 5% of each run, Pallas kernels for 18% -> 17%
where the time goes in v2:
time: 192 us
  waiting for transfers between devices  98.2 us (51%)
  starting transfers between devices  41 us (21%)
  Pallas kernels  32.2 us (17%)
  other arithmetic  10.7 us (6%)
  local copies, waits for them, and re-layouts  7.84 us (4%)
    ppermute x35, waiting for transfers between devices, swap(): return lax.ppermute(array, self.axis, self.pairs)  91.7 us
    ppermute x35, starting transfers between devices, swap(): return lax.ppermute(array, self.axis, self.pairs)  35.6 us
    pallas_call x3, Pallas kernels, grads_of(): pl.pallas_call(functools.partial(chunk_kernel, (kept_at, kept_at, come_at...  32.2 us
    ppermute x3, waiting for transfers between devices, diagonal(): return lax.ppermute(array, 'dp', pairs)  6.54 us
    ppermute x3, starting transfers between devices, diagonal(): return lax.ppermute(array, 'dp', pairs)  5.41 us
  transfers between devices with their start and end apart: 38, of which 19 were waited for; matrix products, arithmetic and copies ran while one was open for 5% of the time, Pallas kernels for 17%

profile of v2, /device:TPU:0, one launch (start us, length us, event | category | flops | bytes accessed | tf_op | source)
XLA Modules:
  0.0 191.5 jit_solution(14519383796496805609)
XLA Ops:
  0.6 4.1 %collective-permute-start.1 = (f32[256,512]{1,0:T(8,128)}, f32[256,512]{1,0:T(8,128)}, u32[]{:S(2)}, u32[]{:S(2)}) collective-permute-start(f32[256,512]{1,0:T(8,128)} %refs_0_.2), channel_id=1, source_target_pairs={{0,16},{2,18},{4,20},{6,22},{8,24},{10,26},{12,28},{14,30},{16,0},... | collective-permute-start | bytes 1572872 | tf_op jit(solution)/shard_map/ppermute | solution.py:31
  12.6 14.1 %collective-permute-done.4 = f32[3,64,512]{2,1,0:T(8,128)S(1)} collective-permute-done((f32[3,64,512]{2,1,0:T(8,128)S(1)}, f32[3,64,512]{2,1,0:T(8,128)S(1)}, u32[]{:S(2)}, u32[]{:S(2)}) %collective-permute-start.4) | collective-permute-done | bytes 393248 | tf_op jit(solution)/shard_map/ppermute | solution.py:31
  26.8 4.2 %collective-permute-done.refs_9_ = f32[256,512]{1,0:T(8,128)} collective-permute-done((f32[256,512]{1,0:T(8,128)}, f32[256,512]{1,0:T(8,128)}, u32[]{:S(2)}, u32[]{:S(2)}) %collective-permute-start) | collective-permute-done | bytes 524320 | tf_op jit(solution)/shard_map/ppermute | solution.py:31
  33.9 2.0 %collective-permute-start.9 = (f32[3,64,512]{2,1,0:T(8,128)S(1)}, f32[3,64,512]{2,1,0:T(8,128)}, u32[]{:S(2)}, u32[]{:S(2)}) collective-permute-start(f32[3,64,512]{2,1,0:T(8,128)S(1)} %pad_maximum_fusion.10), channel_id=1, source_target_pairs={{0,8},{2,10},{4,12},{6,14},{8,0},{10,2},{12,4},{14,6},{16,24},{18,... | collective-permute-start | bytes 1179656 | tf_op jit(solution)/shard_map/ppermute | solution.py:31
  35.9 15.8 %collective-permute-done.6 = f32[448,512]{1,0:T(8,128)} collective-permute-done((f32[448,512]{1,0:T(8,128)S(1)}, f32[448,512]{1,0:T(8,128)}, u32[]{:S(2)}, u32[]{:S(2)}) %collective-permute-start.6) | collective-permute-done | bytes 917536 | tf_op jit(solution)/shard_map/ppermute | solution.py:31
  54.0 1.8 collective-permute-done.5.refs_12_
  64.1 18.3 %collective-permute-done.12 = f32[512,512]{1,0:T(8,128)S(1)} collective-permute-done((f32[512,512]{1,0:T(8,128)S(1)}, f32[512,512]{1,0:T(8,128)S(1)}, u32[]{:S(2)}, u32[]{:S(2)}) %collective-permute-start.12) | collective-permute-done | bytes 1048608 | tf_op jit(solution)/shard_map/ppermute | solution.py:31
  83.3 4.2 %collective-permute-done.10 = f32[2,3,64,384]{3,2,1,0:T(8,128)S(1)} collective-permute-done((f32[2,3,64,384]{3,2,1,0:T(8,128)S(1)}, f32[2,3,64,384]{3,2,1,0:T(8,128)S(1)}, u32[]{:S(2)}, u32[]{:S(2)}) %collective-permute-start.10) | collective-permute-done | bytes 589856 | tf_op jit(solution)/shard_map/ppermute | solution.py:31
  92.2 11.2 %collective-permute-done.19 = f32[2,3,64,128]{3,2,1,0:T(8,128)S(1)} collective-permute-done((f32[2,3,64,128]{3,2,1,0:T(8,128)S(1)}, f32[2,3,64,128]{3,2,1,0:T(8,128)S(1)}, u32[]{:S(2)}, u32[]{:S(2)}) %collective-permute-start.19) | collective-permute-done | bytes 196640 | tf_op jit(solution)/shard_map/ppermute | solution.py:31
  103.4 2.2 %collective-permute-done.15 = f32[2,3,64,256]{3,2,1,0:T(8,128)S(1)} collective-permute-done((f32[2,3,64,256]{3,2,1,0:T(8,128)S(1)}, f32[2,3,64,256]{3,2,1,0:T(8,128)S(1)}, u32[]{:S(2)}, u32[]{:S(2)}) %collective-permute-start.15) | collective-permute-done | bytes 393248 | tf_op jit(solution)/shard_map/ppermute | solution.py:31
  107.3 2.3 %collective-permute-done.20.refs_19_ = f32[4,3,64,256]{3,2,1,0:T(8,128)} collective-permute-done((f32[4,3,64,256]{3,2,1,0:T(8,128)S(1)}, f32[4,3,64,256]{3,2,1,0:T(8,128)}, u32[]{:S(2)}, u32[]{:S(2)}) %collective-permute-start.20) | collective-permute-done | bytes 786464 | tf_op jit(solution)/shard_map/ppermute | solution.py:31
  109.8 15.1 %shard_map.136 = (f32[2,8,64,256]{3,2,1,0:T(8,128)}, f32[2,8,64,256]{3,2,1,0:T(8,128)}) custom-call(s32[3]{0:T(128)S(1)} %pad_add_fusion.mine_ref, f32[256,512]{1,0:T(8,128)S(1)} %copy-done, f32[256,512]{1,0:T(8,128)S(1)} %collective-permute-done.3.refs_1_, f32[256,512]{1,0:T(8,128)S(1)} %collective-permute-done.2.refs_2_, ...), custom_call_target="tpu_custom_call" | custom-call | flops 8053063680 | bytes 8388608 | tf_op jit(solution)/shard_map/pallas_call | solution.py:295
  126.5 2.6 %collective-permute-done.23.refs_19_ = f32[4,3,64,256]{3,2,1,0:T(8,128)} collective-permute-done((f32[4,3,64,256]{3,2,1,0:T(8,128)}, f32[4,3,64,256]{3,2,1,0:T(8,128)}, u32[]{:S(2)}, u32[]{:S(2)}) %collective-permute-start.23) | collective-permute-done | bytes 786464 | tf_op jit(solution)/shard_map/ppermute | solution.py:31
  130.0 2.0 %collective-permute-start.24 = (f32[2,2,2,64,256]{4,3,0,2,1:T(8,128)}, f32[2,2,2,64,256]{4,3,0,2,1:T(8,128)}, u32[]{:S(2)}, u32[]{:S(2)}) collective-permute-start(f32[2,2,2,64,256]{4,3,0,2,1:T(8,128)} %add_bitcast_fusion), channel_id=1, source_target_pairs={{0,8},{2,10},{4,12},{6,14},{8,0},{10,2},{12,4},{14,6},{16,24},{18,... | collective-permute-start | bytes 1572872 | tf_op jit(solution)/shard_map/ppermute | solution.py:31
  132.1 8.7 %shard_map.137 = (f32[1,8,64,256]{3,2,1,0:T(8,128)S(1)}, f32[1,8,64,256]{3,2,1,0:T(8,128)S(1)}) custom-call(s32[3]{0:T(128)S(1)} %pad_add_fusion.mine_ref, f32[256,512]{1,0:T(8,128)S(1)} %copy-done, f32[256,512]{1,0:T(8,128)} %copy-done.2, f32[256,512]{1,0:T(8,128)} %copy-done.1, f32[256,512]{1,0:T(8,128)} %collective-permute-done.7.refs_3_, ...), custom_call_target="tpu_custom_call" | custom-call | flops 4026531840 | bytes 8388608 | tf_op jit(solution)/shard_map/pallas_call | solution.py:295
  140.8 3.8 %collective-permute-done.24 = f32[2,2,2,64,256]{4,3,0,2,1:T(8,128)} collective-permute-done((f32[2,2,2,64,256]{4,3,0,2,1:T(8,128)}, f32[2,2,2,64,256]{4,3,0,2,1:T(8,128)}, u32[]{:S(2)}, u32[]{:S(2)}) %collective-permute-start.24) | collective-permute-done | bytes 524320 | tf_op jit(solution)/shard_map/ppermute | solution.py:31
  145.8 1.9 collective-permute-done.25
  147.7 1.8 collective-permute-start.29
  153.9 8.4 %shard_map.138 = (f32[1,8,64,256]{3,2,1,0:T(8,128)S(1)}, f32[1,8,64,256]{3,2,1,0:T(8,128)S(1)}) custom-call(s32[3]{0:T(128)S(1)} %pad_add_fusion.mine_ref, f32[256,512]{1,0:T(8,128)S(1)} %copy-done, f32[256,512]{1,0:T(8,128)} %copy-done.2, f32[256,512]{1,0:T(8,128)} %copy-done.1, f32[256,512]{1,0:T(8,128)} %collective-permute-done.7.refs_3_, ...), custom_call_target="tpu_custom_call" | custom-call | flops 4026531840 | bytes 8388608 | tf_op jit(solution)/shard_map/pallas_call | solution.py:295
  165.6 1.9 collective-permute-done.30
  172.2 3.5 %collective-permute-done.32 = f32[1,64,256]{2,1,0:T(8,128)S(1)} collective-permute-done((f32[1,64,256]{2,1,0:T(8,128)S(1)}, f32[1,64,256]{2,1,0:T(8,128)S(1)}, u32[]{:S(2)}, u32[]{:S(2)}) %collective-permute-start.32) | collective-permute-done | bytes 65568 | tf_op jit(solution)/shard_map/ppermute | solution.py:31
  175.7 4.0 %collective-permute-done.33 = f32[1,64,256]{2,1,0:T(8,128)S(1)} collective-permute-done((f32[1,64,256]{2,1,0:T(8,128)S(1)}, f32[1,64,256]{2,1,0:T(8,128)S(1)}, u32[]{:S(2)}, u32[]{:S(2)}) %collective-permute-start.33) | collective-permute-done | bytes 65568 | tf_op jit(solution)/shard_map/ppermute | solution.py:211
  181.7 2.5 %collective-permute-start.37 = (f32[1,64,256]{2,1,0:T(8,128)S(1)}, f32[1,64,256]{2,1,0:T(8,128)S(1)}, u32[]{:S(2)}, u32[]{:S(2)}) collective-permute-start(f32[1,64,256]{2,1,0:T(8,128)S(1)} %get-tuple-element.345), channel_id=1, source_target_pairs={{0,20},{2,22},{4,16},{6,18},{8,28},{10,30},{12,24},{14,26},{16,4},... | collective-permute-start | bytes 196616 | tf_op jit(solution)/shard_map/ppermute | solution.py:211
  184.4 2.3 %collective-permute-done.36 = f32[1,64,256]{2,1,0:T(8,128)S(1)} collective-permute-done((f32[1,64,256]{2,1,0:T(8,128)S(1)}, f32[1,64,256]{2,1,0:T(8,128)S(1)}, u32[]{:S(2)}, u32[]{:S(2)}) %collective-permute-start.36) | collective-permute-done | bytes 65568 | tf_op jit(solution)/shard_map/ppermute | solution.py:31
  (178 shorter events, 51.3 us)
Async XLA Ops:
  0.6 30.3 %collective-permute-start.1 = (f32[256,512]{1,0:T(8,128)}, f32[256,512]{1,0:T(8,128)}, u32[]{:S(2)}, u32[]{:S(2)}) collective-permute-start(f32[256,512]{1,0:T(8,128)} %refs_0_.2), channel_id=1, source_target_pairs={{0,16},{2,18},{4,20},{6,22},{8,24},{10,26},{12,28},{14,30},{16,0},... | collective-permute-start | bytes 1572872 | tf_op jit(solution)/shard_map/ppermute | solution.py:31
  4.7 26.2 %collective-permute-start.2 = (f32[256,512]{1,0:T(8,128)}, f32[256,512]{1,0:T(8,128)S(1)}, u32[]{:S(2)}, u32[]{:S(2)}) collective-permute-start(f32[256,512]{1,0:T(8,128)} %refs_0_.2), channel_id=1, source_target_pairs={{0,4},{2,6},{4,0},{6,2},{8,12},{10,14},{12,8},{14,10},{16,20},{18,... | collective-permute-start | bytes 1572872 | tf_op jit(solution)/shard_map/ppermute | solution.py:31
  6.3 24.7 %collective-permute-start.3 = (f32[256,512]{1,0:T(8,128)}, f32[256,512]{1,0:T(8,128)S(1)}, u32[]{:S(2)}, u32[]{:S(2)}) collective-permute-start(f32[256,512]{1,0:T(8,128)} %refs_0_.2), channel_id=1, source_target_pairs={{0,1},{1,0},{2,3},{3,2},{4,5},{5,4},{6,7},{7,6},{8,9},{9,8},{10,11... | collective-permute-start | bytes 1572872 | tf_op jit(solution)/shard_map/ppermute | solution.py:31
  7.7 23.2 %collective-permute-start = (f32[256,512]{1,0:T(8,128)}, f32[256,512]{1,0:T(8,128)}, u32[]{:S(2)}, u32[]{:S(2)}) collective-permute-start(f32[256,512]{1,0:T(8,128)} %refs_8_.2), channel_id=1, source_target_pairs={{0,1},{1,0},{2,3},{3,2},{4,5},{5,4},{6,7},{7,6},{8,9},{9,8},{10,11... | collective-permute-start | bytes 1572872 | tf_op jit(solution)/shard_map/ppermute | solution.py:31
  10.9 15.9 %collective-permute-start.4 = (f32[3,64,512]{2,1,0:T(8,128)S(1)}, f32[3,64,512]{2,1,0:T(8,128)S(1)}, u32[]{:S(2)}, u32[]{:S(2)}) collective-permute-start(f32[3,64,512]{2,1,0:T(8,128)S(1)} %pad_maximum_fusion.11), channel_id=1, source_target_pairs={{0,4},{2,6},{4,0},{6,2},{8,12},{10,14},{12,8},{14,10},{16,20},{18,... | collective-permute-start | bytes 1179656 | tf_op jit(solution)/shard_map/ppermute | solution.py:31
  30.9 20.8 %collective-permute-start.6 = (f32[448,512]{1,0:T(8,128)S(1)}, f32[448,512]{1,0:T(8,128)}, u32[]{:S(2)}, u32[]{:S(2)}) collective-permute-start(f32[448,512]{1,0:T(8,128)S(1)} %pad_maximum_fusion.2), channel_id=1, source_target_pairs={{0,4},{2,6},{4,0},{6,2},{8,12},{10,14},{12,8},{14,10},{16,20},{18,... | collective-permute-start | bytes 2752520 | tf_op jit(solution)/shard_map/ppermute | solution.py:31
  31.5 24.3 %collective-permute-start.5 = (f32[256,512]{1,0:T(8,128)}, f32[256,512]{1,0:T(8,128)}, u32[]{:S(2)}, u32[]{:S(2)}) collective-permute-start(f32[256,512]{1,0:T(8,128)} %refs_8_.2), channel_id=1, source_target_pairs={{0,16},{2,18},{4,20},{6,22},{8,24},{10,26},{12,28},{14,30},{16,0},... | collective-permute-start | bytes 1572872 | tf_op jit(solution)/shard_map/ppermute | solution.py:31
  31.9 24.0 %collective-permute-start.7 = (f32[256,512]{1,0:T(8,128)S(1)}, f32[256,512]{1,0:T(8,128)}, u32[]{:S(2)}, u32[]{:S(2)}) collective-permute-start(f32[256,512]{1,0:T(8,128)S(1)} %collective-permute-done.2.refs_2_), channel_id=1, source_target_pairs={{0,1},{1,0},{2,3},{3,2},{4,5},{5,4},{6,7},{7,6},{8,9},{9,8},{10,11... | collective-permute-start | bytes 1572872 | tf_op jit(solution)/shard_map/ppermute | solution.py:31
  33.4 22.5 %collective-permute-start.8 = (f32[256,512]{1,0:T(8,128)}, f32[256,512]{1,0:T(8,128)}, u32[]{:S(2)}, u32[]{:S(2)}) collective-permute-start(f32[256,512]{1,0:T(8,128)} %collective-permute-done.1.refs_4_), channel_id=1, source_target_pairs={{0,1},{1,0},{2,3},{3,2},{4,5},{5,4},{6,7},{7,6},{8,9},{9,8},{10,11... | collective-permute-start | bytes 1572872 | tf_op jit(solution)/shard_map/ppermute | solution.py:31
  33.9 20.1 %collective-permute-start.9 = (f32[3,64,512]{2,1,0:T(8,128)S(1)}, f32[3,64,512]{2,1,0:T(8,128)}, u32[]{:S(2)}, u32[]{:S(2)}) collective-permute-start(f32[3,64,512]{2,1,0:T(8,128)S(1)} %pad_maximum_fusion.10), channel_id=1, source_target_pairs={{0,8},{2,10},{4,12},{6,14},{8,0},{10,2},{12,4},{14,6},{16,24},{18,... | collective-permute-start | bytes 1179656 | tf_op jit(solution)/shard_map/ppermute | solution.py:31
  55.9 27.5 %collective-permute-start.13 = (f32[256,512]{1,0:T(8,128)}, f32[256,512]{1,0:T(8,128)S(1)}, u32[]{:S(2)}, u32[]{:S(2)}) collective-permute-start(f32[256,512]{1,0:T(8,128)} %collective-permute-done.5.refs_12_), channel_id=1, source_target_pairs={{0,1},{1,0},{2,3},{3,2},{4,5},{5,4},{6,7},{7,6},{8,9},{9,8},{10,11... | collective-permute-start | bytes 1572872 | tf_op jit(solution)/shard_map/ppermute | solution.py:31
  58.6 23.8 %collective-permute-start.12 = (f32[512,512]{1,0:T(8,128)S(1)}, f32[512,512]{1,0:T(8,128)S(1)}, u32[]{:S(2)}, u32[]{:S(2)}) collective-permute-start(f32[512,512]{1,0:T(8,128)S(1)} %pad_maximum_fusion.1), channel_id=1, source_target_pairs={{0,4},{2,6},{4,0},{6,2},{8,12},{10,14},{12,8},{14,10},{16,20},{18,... | collective-permute-start | bytes 3145736 | tf_op jit(solution)/shard_map/ppermute | solution.py:31
  60.3 27.2 %collective-permute-start.10 = (f32[2,3,64,384]{3,2,1,0:T(8,128)S(1)}, f32[2,3,64,384]{3,2,1,0:T(8,128)S(1)}, u32[]{:S(2)}, u32[]{:S(2)}) collective-permute-start(f32[2,3,64,384]{3,2,1,0:T(8,128)S(1)} %pad_maximum_fusion.7), channel_id=1, source_target_pairs={{0,16},{2,18},{4,20},{6,22},{8,24},{10,26},{12,28},{14,30},{16,0},... | collective-permute-start | bytes 1769480 | tf_op jit(solution)/shard_map/ppermute | solution.py:31
  62.0 21.3 %collective-permute-start.11 = (f32[256,512]{1,0:T(8,128)S(1)}, f32[256,512]{1,0:T(8,128)S(1)}, u32[]{:S(2)}, u32[]{:S(2)}) collective-permute-start(f32[256,512]{1,0:T(8,128)S(1)} %slice.208.refs_10_), channel_id=1, source_target_pairs={{0,1},{1,0},{2,3},{3,2},{4,5},{5,4},{6,7},{7,6},{8,9},{9,8},{10,11... | collective-permute-start | bytes 1572872 | tf_op jit(solution)/shard_map/ppermute | solution.py:31
  62.5 20.8 %collective-permute-start.14 = (f32[3,64,512]{2,1,0:T(8,128)S(1)}, f32[3,64,512]{2,1,0:T(8,128)S(1)}, u32[]{:S(2)}, u32[]{:S(2)}) collective-permute-start(f32[3,64,512]{2,1,0:T(8,128)S(1)} %copy-done.16), channel_id=1, source_target_pairs={{0,8},{2,10},{4,12},{6,14},{8,0},{10,2},{12,4},{14,6},{16,24},{18,... | collective-permute-start | bytes 1179656 | tf_op jit(solution)/shard_map/ppermute | solution.py:31
  89.2 16.4 %collective-permute-start.18 = (f32[4,3,64,512]{3,2,1,0:T(8,128)S(1)}, f32[4,3,64,512]{3,2,1,0:T(8,128)S(1)}, u32[]{:S(2)}, u32[]{:S(2)}) collective-permute-start(f32[4,3,64,512]{3,2,1,0:T(8,128)S(1)} %bitcast.317), channel_id=1, source_target_pairs={{0,2},{2,0},{4,6},{6,4},{8,10},{10,8},{12,14},{14,12},{16,18},{18,... | collective-permute-start | bytes 4718600 | tf_op jit(solution)/shard_map/ppermute | solution.py:31
  89.3 16.3 %collective-permute-start.16 = (f32[256,512]{1,0:T(8,128)S(1)}, f32[256,512]{1,0:T(8,128)S(1)}, u32[]{:S(2)}, u32[]{:S(2)}) collective-permute-start(f32[256,512]{1,0:T(8,128)S(1)} %get-tuple-element.313.refs_14_), channel_id=1, source_target_pairs={{0,1},{1,0},{2,3},{3,2},{4,5},{5,4},{6,7},{7,6},{8,9},{9,8},{10,11... | collective-permute-start | bytes 1572872 | tf_op jit(solution)/shard_map/ppermute | solution.py:31
  89.9 15.7 %collective-permute-start.17 = (f32[256,512]{1,0:T(8,128)}, f32[256,512]{1,0:T(8,128)S(1)}, u32[]{:S(2)}, u32[]{:S(2)}) collective-permute-start(f32[256,512]{1,0:T(8,128)} %collective-permute-done.8.refs_5_), channel_id=1, source_target_pairs={{0,4},{2,6},{4,0},{6,2},{8,12},{10,14},{12,8},{14,10},{16,20},{18,... | collective-permute-start | bytes 1572872 | tf_op jit(solution)/shard_map/ppermute | solution.py:31
  90.4 15.2 %collective-permute-start.15 = (f32[2,3,64,256]{3,2,1,0:T(8,128)S(1)}, f32[2,3,64,256]{3,2,1,0:T(8,128)S(1)}, u32[]{:S(2)}, u32[]{:S(2)}) collective-permute-start(f32[2,3,64,256]{3,2,1,0:T(8,128)S(1)} %slice.164), channel_id=1, source_target_pairs={{0,8},{2,10},{4,12},{6,14},{8,0},{10,2},{12,4},{14,6},{16,24},{18,... | collective-permute-start | bytes 1179656 | tf_op jit(solution)/shard_map/ppermute | solution.py:31
  109.7 15.2 %collective-permute-start.21 = (f32[2,3,64,256]{3,2,1,0:T(8,128)S(1)}, f32[2,3,64,256]{3,2,1,0:T(8,128)S(1)}, u32[]{:S(2)}, u32[]{:S(2)}) collective-permute-start(f32[2,3,64,256]{3,2,1,0:T(8,128)S(1)} %constant_dynamic-update-slice_fusion), channel_id=1, source_target_pairs={{0,8},{2,10},{4,12},{6,14},{8,0},{10,2},{12,4},{14,6},{16,24},{18,... | collective-permute-start | bytes 1179656 | tf_op jit(solution)/shard_map/ppermute | solution.py:31
  130.0 14.5 %collective-permute-start.24 = (f32[2,2,2,64,256]{4,3,0,2,1:T(8,128)}, f32[2,2,2,64,256]{4,3,0,2,1:T(8,128)}, u32[]{:S(2)}, u32[]{:S(2)}) collective-permute-start(f32[2,2,2,64,256]{4,3,0,2,1:T(8,128)} %add_bitcast_fusion), channel_id=1, source_target_pairs={{0,8},{2,10},{4,12},{6,14},{8,0},{10,2},{12,4},{14,6},{16,24},{18,... | collective-permute-start | bytes 1572872 | tf_op jit(solution)/shard_map/ppermute | solution.py:31
  147.7 17.7 %collective-permute-start.29 = (f32[1,2,2,64,256]{4,3,2,1,0:T(8,128)S(1)}, f32[1,2,2,64,256]{4,3,2,1,0:T(8,128)S(1)}, u32[]{:S(2)}, u32[]{:S(2)}) collective-permute-start(f32[1,2,2,64,256]{4,3,2,1,0:T(8,128)S(1)} %add_bitcast_fusion.2), channel_id=1, source_target_pairs={{0,8},{2,10},{4,12},{6,14},{8,0},{10,2},{12,4},{14,6},{16,24},{18,... | collective-permute-start | bytes 786440 | tf_op jit(solution)/shard_map/ppermute | solution.py:31
  151.1 12.9 %collective-permute-start.27 = (f32[2,64,256]{2,1,0:T(8,128)S(1)}, f32[2,64,256]{2,1,0:T(8,128)S(1)}, u32[]{:S(2)}, u32[]{:S(2)}) collective-permute-start(f32[2,64,256]{2,1,0:T(8,128)S(1)} %get-tuple-element.322), channel_id=1, source_target_pairs={{0,16},{2,18},{4,20},{6,22},{8,24},{10,26},{12,28},{14,30},{16,0},... | collective-permute-start | bytes 393224 | tf_op jit(solution)/shard_map/ppermute | solution.py:31
  152.3 13.1 %collective-permute-start.28 = (f32[2,64,256]{2,1,0:T(8,128)S(1)}, f32[2,64,256]{2,1,0:T(8,128)S(1)}, u32[]{:S(2)}, u32[]{:S(2)}) collective-permute-start(f32[2,64,256]{2,1,0:T(8,128)S(1)} %get-tuple-element.323), channel_id=1, source_target_pairs={{0,20},{2,22},{4,16},{6,18},{8,28},{10,30},{12,24},{14,26},{16,4},... | collective-permute-start | bytes 393224 | tf_op jit(solution)/shard_map/ppermute | solution.py:211
  (39 other events, 342.7 us)
